TPU v7x, 256 devices: a whole 4x4x8 slice. The times are simulated.
256 devices in a mesh: dom: 64 (over y_hi, z, x), rep: 4 (over y_lo, core).
Axes of the slice: x: 4, y: 4 (y_hi: 2, y_lo: 2; y = y_hi * 2 + y_lo), z: 8, core: 2. Of those that a mesh axis runs over, the one named last changes fastest.
Arguments:
- entity_table: float32 [262144, 400], P('dom'), may hold values from -2.5 to 2.5
- entity_state: float32 [262144], P('dom'), may hold values from 0.02 to 0.2
- relation_table: float32 [1300, 400], replicated, may hold values from -1 to 1
- relation_state: float32 [1300], replicated, may hold values from 1 to 10
- source_rows: int32 [2, 64, 1024], P(None, 'dom', 'rep'), may hold values from 0 to 4095
- target_rows: int32 [2, 64, 1024], P(None, 'dom', 'rep'), may hold values from 0 to 4095
- relation_ids: int32 [2, 64, 1024], P(None, 'dom', 'rep'), may hold values from 0 to 1299
- live_counts: int32 [2, 64, 4], P(None, 'dom', 'rep'), may hold values from 64 to 256, as said below
Outputs:
- new_entities: float32 [262144, 400], P(('dom', 'rep'))
- new_entity_state: float32 [262144], P(('dom', 'rep'))
- new_relations: float32 [1300, 400], replicated
- new_relation_state: float32 [1300], replicated
Inputs may be any that keep to these rules, and one draw needn't show every extreme that they name: live_counts[t, p, c]: live slots, the first ones, of block c of bucket p in round t; in each round some block has all 256 live.
All inputs are finite; a program needn't handle non-finite values.
Results may differ from a plain program's by a relative error of at most 0.0048.
Values may be sent and summed in bfloat16 or wider, within the bound.
A program may use at most 128 MiB of HBM per device.

v0:
```python
import jax
import jax.numpy as jnp
from jax import lax
from jax.sharding import PartitionSpec as P

learning_rate = 0.2
epsilon = 1e-06


def passed_along(value, axis, by):
    size = lax.axis_size(axis)
    return lax.ppermute(value, axis, [(i, (i + by) % size) for i in range(size)])


def one_hot_rows(indices, first_row, row_count):
    columns = first_row + jnp.arange(row_count, dtype=jnp.int32)
    return (indices[:, None] == columns[None, :]).astype(jnp.bfloat16)


def lookup(indices, table_b):
    indicator = one_hot_rows(indices, 0, table_b.shape[0])
    return jnp.dot(indicator, table_b, preferred_element_type=jnp.float32).astype(jnp.bfloat16)


def spread_rows(indices, first_row, row_count, values):
    indicator = one_hot_rows(indices, first_row, row_count)
    return lax.dot_general(
        indicator, values, (((0,), (0,)), ((), ())), preferred_element_type=jnp.float32
    )


def group_terms(sources, relations, targets, live_count):
    half_width = sources.shape[1] // 2
    src_f = sources.astype(jnp.float32)
    rel_f = relations.astype(jnp.float32)
    src_re, src_im = (src_f[:, :half_width], src_f[:, half_width:])
    rel_re, rel_im = (rel_f[:, :half_width], rel_f[:, half_width:])
    queries = jnp.concatenate(
        [src_re * rel_re - src_im * rel_im, src_re * rel_im + src_im * rel_re], axis=1
    ).astype(jnp.bfloat16)
    scores = lax.dot_general(
        queries, targets, (((1,), (1,)), ((), ())), preferred_element_type=jnp.float32
    )
    slot_ids = jnp.arange(sources.shape[0], dtype=jnp.int32)
    is_live = slot_ids < live_count
    exp_terms = jnp.where(is_live[None, :], jnp.exp(scores), jnp.float32(0.0))
    probability = exp_terms / jnp.sum(exp_terms, axis=1, keepdims=True)
    diagonal = (slot_ids[:, None] == slot_ids[None, :]).astype(jnp.float32)
    coeffs = jnp.where(is_live[:, None], probability - diagonal, jnp.float32(0.0)).astype(
        jnp.bfloat16
    )
    d_queries = jnp.dot(coeffs, targets, preferred_element_type=jnp.float32)
    d_keys = lax.dot_general(
        coeffs, queries, (((0,), (0,)), ((), ())), preferred_element_type=jnp.float32
    ).astype(jnp.bfloat16)
    dq_re, dq_im = (d_queries[:, :half_width], d_queries[:, half_width:])
    d_src = jnp.concatenate(
        [dq_re * rel_re + dq_im * rel_im, dq_im * rel_re - dq_re * rel_im], axis=1
    ).astype(jnp.bfloat16)
    d_rel = jnp.concatenate(
        [dq_re * src_re + dq_im * src_im, dq_im * src_re - dq_re * src_im], axis=1
    ).astype(jnp.bfloat16)
    return (d_src, d_rel, d_keys)


def row_adagrad(table_rows, adagrad_state, gradients):
    new_state = adagrad_state + jnp.mean(gradients * gradients, axis=1)
    return (
        table_rows - learning_rate * gradients / (jnp.sqrt(new_state)[:, None] + epsilon),
        new_state,
    )


def per_device(
    entity_table,
    entity_state,
    relation_table,
    relation_state,
    source_rows,
    target_rows,
    relation_ids,
    live_counts,
):
    rows_all = entity_table.shape[0]
    rep_total = lax.axis_size("rep")
    dom_total = lax.axis_size("dom")
    share_rows = rows_all // rep_total
    rep_index = lax.axis_index("rep")
    own_rows = lax.dynamic_slice_in_dim(entity_table, rep_index * share_rows, share_rows, 0)
    own_state = lax.dynamic_slice_in_dim(entity_state, rep_index * share_rows, share_rows, 0)
    dense_table = entity_table.astype(jnp.bfloat16)
    relation_b = relation_table.astype(jnp.bfloat16)
    relation_total = jnp.zeros(relation_table.shape, jnp.float32)
    for round_idx in range(2):
        offset = 1 if round_idx == 0 else dom_total // 2
        sources = source_rows[round_idx, 0]
        target_ids = target_rows[round_idx, 0]
        relation_kind = relation_ids[round_idx, 0]
        live_count = live_counts[round_idx, 0, 0]
        source_b = lookup(sources, dense_table)
        relation_rows = lookup(relation_kind, relation_b)
        partner_table = passed_along(dense_table, "dom", -offset)
        target_b = lookup(target_ids, partner_table)
        d_src, d_rel, d_keys = group_terms(source_b, relation_rows, target_b, live_count)
        relation_part = spread_rows(relation_kind, 0, relation_table.shape[0], d_rel)
        relation_total = relation_total + lax.psum(relation_part, ("dom", "rep"))
        block_back = passed_along(spread_rows(target_ids, 0, rows_all, d_keys), "dom", offset)
        own_part = spread_rows(sources, jnp.int32(0), share_rows * lax.axis_size("rep"), d_src)
        row_gradients = lax.psum_scatter(
            own_part + block_back, "rep", scatter_dimension=0, tiled=True
        )
        own_rows, own_state = row_adagrad(own_rows, own_state, row_gradients)
        if round_idx == 0:
            dense_table = lax.all_gather(own_rows.astype(jnp.bfloat16), "rep", axis=0, tiled=True)
    new_relations, new_relation_state = row_adagrad(relation_table, relation_state, relation_total)
    return (own_rows, own_state, new_relations, new_relation_state)


def solution(mesh):
    in_specs = (
        P("dom", None),
        P("dom"),
        P(),
        P(),
        P(None, "dom", "rep"),
        P(None, "dom", "rep"),
        P(None, "dom", "rep"),
        P(None, "dom", "rep"),
    )
    out_specs = (P(("dom", "rep"), None), P(("dom", "rep")), P(), P())
    return jax.shard_map(
        per_device, mesh=mesh, in_specs=in_specs, out_specs=out_specs, check_vma=False
    )
```

profile of v0, /device:TPU:1, one launch (start us, length us, event | category | flops | bytes accessed | tf_op | source)
XLA Modules:
  0.0 881.6 jit_solution(18265589328555770349)
XLA Ops:
  7.3 3.5 convert_element_type.75
  10.7 11.3 %collective-permute-start = (bf16[4096,400]{0,1:T(8,128)(2,1)S(1)}, bf16[4096,400]{0,1:T(8,128)(2,1)S(1)}, u32[]{:S(2)}, u32[]{:S(2)}) collective-permute-start(bf16[4096,400]{0,1:T(8,128)(2,1)S(1)} %convert_element_type.75), channel_id=1, source_target_pairs={{0,252},{4,0},{8,4},{12,8},{16,12},{20,16},{24,20},{28,24},{32,28}... | collective-permute-start | bytes 9830408 | tf_op jit(solution)/shard_map/ppermute | solution.py:12
  25.9 65.7 %collective-permute-done = bf16[4096,400]{0,1:T(8,128)(2,1)S(1)} collective-permute-done((bf16[4096,400]{0,1:T(8,128)(2,1)S(1)}, bf16[4096,400]{0,1:T(8,128)(2,1)S(1)}, u32[]{:S(2)}, u32[]{:S(2)}) %collective-permute-start) | collective-permute-done | bytes 3276832 | tf_op jit(solution)/shard_map/ppermute | solution.py:12
  93.8 4.8 fusion.3
  99.9 146.7 %collective-permute-done.1 = f32[4096,400]{0,1:T(8,128)S(1)} collective-permute-done((f32[4096,400]{0,1:T(8,128)}, f32[4096,400]{0,1:T(8,128)S(1)}, u32[]{:S(2)}, u32[]{:S(2)}) %collective-permute-start.1) | collective-permute-done | bytes 6553632 | tf_op jit(solution)/shard_map/ppermute | solution.py:12
  246.6 4.1 convolution_add_fusion.1
  250.7 61.5 %reduce-scatter.3.cloned.1.call-done = f32[1024,400]{0,1:T(8,128)} async-done(((f32[4096,400]{0,1:T(8,128)}), f32[1024,400]{0,1:T(8,128)}) %reduce-scatter.3.cloned.1.call-update) | async-done | bytes 1638416 | tf_op jit(solution)/shard_map/reduce_scatter | solution.py:109
  312.2 1.7 multiply_reduce_fusion.2
  314.2 2.6 fusion.69
  316.8 42.7 %all-gather.2.cloned.1.call-done = bf16[4096,400]{0,1:T(8,128)(2,1)} async-done(((bf16[1024,400]{0,1:T(8,128)(2,1)}), bf16[4096,400]{0,1:T(8,128)(2,1)}) %all-gather.2.cloned.1.call-update) | async-done | bytes 3276816 | tf_op jit(solution)/shard_map/all_gather | solution.py:114
  359.5 2.4 collective-permute-start.2
  363.3 3.1 fusion.25
  366.5 67.3 %collective-permute-done.2 = bf16[4096,400]{0,1:T(8,128)(2,1)S(1)} collective-permute-done((bf16[4096,400]{0,1:T(8,128)(2,1)}, bf16[4096,400]{0,1:T(8,128)(2,1)S(1)}, u32[]{:S(2)}, u32[]{:S(2)}) %collective-permute-start.2) | collective-permute-done | bytes 3276832 | tf_op jit(solution)/shard_map/ppermute | solution.py:12
  436.8 5.1 fusion
  441.9 2.4 collective-permute-start.3
  445.4 2.0 convolution_add_fusion.2
  447.5 140.9 %collective-permute-done.3 = f32[4096,400]{0,1:T(8,128)} collective-permute-done((f32[4096,400]{0,1:T(8,128)}, f32[4096,400]{0,1:T(8,128)}, u32[]{:S(2)}, u32[]{:S(2)}) %collective-permute-start.3) | collective-permute-done | bytes 6553632 | tf_op jit(solution)/shard_map/ppermute | solution.py:12
  588.4 6.9 convolution_add_fusion
  595.3 203.7 %all-reduce.2.cloned.1.call-done = f32[1300,400]{0,1:T(8,128)} async-done(((f32[1300,400]{0,1:T(8,128)}), f32[1300,400]{0,1:T(8,128)}) %all-reduce.2.cloned.1.call-update) | async-done | bytes 2080016 | tf_op jit(solution)/shard_map/psum | solution.py:106
  799.1 2.0 multiply_reduce_fusion
  801.7 1.7 divide_subtract_fusion
  803.4 65.9 %reduce-scatter.5.cloned.1.call-done = f32[1024,400]{0,1:T(8,128)} async-done(((f32[4096,400]{0,1:T(8,128)}), f32[1024,400]{0,1:T(8,128)}) %reduce-scatter.5.cloned.1.call-update) | async-done | bytes 1638416 | tf_op jit(solution)/shard_map/reduce_scatter | solution.py:109
  869.2 1.6 multiply_reduce_fusion.1
  871.4 3.6 divide_subtract_fusion.1
  (66 shorter events, 14.1 us)
Async XLA Ops:
  7.2 14.9 %copy-start.12 = (s32[2,1,1]{0,2,1:T(1,128)S(1)}, s32[2,1,1]{0,2,1:T(1,128)}, u32[]{:S(2)}) copy-start(s32[2,1,1]{0,2,1:T(1,128)} %param.15) | copy-start | bytes 28
  7.2 16.2 %copy-start.9 = (s32[2,1,256]{2,1,0:T(1,128)S(1)}, s32[2,1,256]{2,1,0:T(1,128)}, u32[]{:S(2)}) copy-start(s32[2,1,256]{2,1,0:T(1,128)} %param.13) | copy-start | bytes 6148
  7.2 16.8 %copy-start.10 = (s32[2,1,256]{2,1,0:T(1,128)S(1)}, s32[2,1,256]{2,1,0:T(1,128)}, u32[]{:S(2)}) copy-start(s32[2,1,256]{2,1,0:T(1,128)} %param.14) | copy-start | bytes 6148
  7.2 16.7 %copy-start.11 = (s32[2,1,256]{2,1,0:T(1,128)S(1)}, s32[2,1,256]{2,1,0:T(1,128)}, u32[]{:S(2)}) copy-start(s32[2,1,256]{2,1,0:T(1,128)} %param.12) | copy-start | bytes 6148
  7.2 16.8 %copy-start = (f32[1300,400]{0,1:T(8,128)S(1)}, f32[1300,400]{0,1:T(8,128)}, u32[]{:S(2)}) copy-start(f32[1300,400]{0,1:T(8,128)} %param.10) | copy-start | bytes 6240004
  7.2 305.0 %reduce-scatter.3.cloned.1.call-start = ((), (), s32[]{:S(2)}) async-start(), calls=%async_computation.2 | async-start | bytes 8192000 | tf_op jit(solution)/shard_map/reduce_scatter | solution.py:109
  10.7 80.9 %collective-permute-start = (bf16[4096,400]{0,1:T(8,128)(2,1)S(1)}, bf16[4096,400]{0,1:T(8,128)(2,1)S(1)}, u32[]{:S(2)}, u32[]{:S(2)}) collective-permute-start(bf16[4096,400]{0,1:T(8,128)(2,1)S(1)} %convert_element_type.75), channel_id=1, source_target_pairs={{0,252},{4,0},{8,4},{12,8},{16,12},{20,16},{24,20},{28,24},{32,28}... | collective-permute-start | bytes 9830408 | tf_op jit(solution)/shard_map/ppermute | solution.py:12
  23.4 69.5 %copy-start.13 = (pred[256]{0:T(512)(128)(4,1)}, pred[256]{0:T(512)(128)(4,1)S(1)}, u32[]{:S(2)}) copy-start(pred[256]{0:T(512)(128)(4,1)S(1)} %iota_compare_fusion.40) | copy-start | bytes 772
  23.9 67.7 %copy-start.8 = (s32[1,1,256]{2,1,0:T(1,128)}, s32[1,1,256]{2,1,0:T(1,128)S(1)}, u32[]{:S(2)}) copy-start(s32[1,1,256]{2,1,0:T(1,128)S(1)} %get-tuple-element.28) | copy-start | bytes 3076
  92.9 0.9 copy-start.16
  98.6 148.0 %collective-permute-start.1 = (f32[4096,400]{0,1:T(8,128)}, f32[4096,400]{0,1:T(8,128)S(1)}, u32[]{:S(2)}, u32[]{:S(2)}) collective-permute-start(f32[4096,400]{0,1:T(8,128)} %fusion.3), channel_id=1, source_target_pairs={{0,4},{4,8},{8,12},{12,16},{16,20},{20,24},{24,28},{28,32},{32,36}... | collective-permute-start | bytes 19660808 | tf_op jit(solution)/shard_map/ppermute | solution.py:12
  250.7 63.3 %copy-start.6 = (f32[4096]{0:T(1024)S(1)}, f32[4096]{0:T(1024)}, u32[]{:S(2)}) copy-start(f32[4096]{0:T(1024)} %param.9) | copy-start | bytes 49156
  250.7 108.9 %all-gather.2.cloned.1.call-start = ((), (), s32[]{:S(2)}) async-start(), calls=%async_computation.3 | async-start | bytes 4096000 | tf_op jit(solution)/shard_map/all_gather | solution.py:114
  312.2 1.9 copy-start.1
  316.8 482.3 %all-reduce.2.cloned.1.call-start = ((), (), s32[]{:S(2)}) async-start(), calls=%async_computation.5 | async-start | bytes 4505600 | tf_op jit(solution)/shard_map/psum | solution.py:106
  359.5 74.3 %collective-permute-start.2 = (bf16[4096,400]{0,1:T(8,128)(2,1)}, bf16[4096,400]{0,1:T(8,128)(2,1)S(1)}, u32[]{:S(2)}, u32[]{:S(2)}) collective-permute-start(bf16[4096,400]{0,1:T(8,128)(2,1)} %all-gather.2.cloned.1.call-done), channel_id=1, source_target_pairs={{0,128},{4,132},{8,136},{12,140},{16,144},{20,148},{24,152},{28,15... | collective-permute-start | bytes 9830408 | tf_op jit(solution)/shard_map/ppermute | solution.py:12
  363.3 70.6 %copy-start.7 = (s32[1,1,256]{2,1,0:T(1,128)S(1)}, s32[1,1,256]{2,1,0:T(1,128)}, u32[]{:S(2)}) copy-start(s32[1,1,256]{2,1,0:T(1,128)} %get-tuple-element.29) | copy-start | bytes 3076
  441.9 3.1 copy-start.4
  441.9 3.1 copy-start.15
  441.9 146.5 %collective-permute-start.3 = (f32[4096,400]{0,1:T(8,128)}, f32[4096,400]{0,1:T(8,128)}, u32[]{:S(2)}, u32[]{:S(2)}) collective-permute-start(f32[4096,400]{0,1:T(8,128)} %fusion), channel_id=1, source_target_pairs={{0,128},{4,132},{8,136},{12,140},{16,144},{20,148},{24,152},{28,15... | collective-permute-start | bytes 19660808 | tf_op jit(solution)/shard_map/ppermute | solution.py:12
  447.4 421.8 %reduce-scatter.5.cloned.1.call-start = ((), (), s32[]{:S(2)}) async-start(), calls=%async_computation.4 | async-start | bytes 8192000 | tf_op jit(solution)/shard_map/reduce_scatter | solution.py:109
  595.3 205.7 %copy-start.5 = (f32[1300]{0:T(1024)S(1)}, f32[1300]{0:T(1024)}, u32[]{:S(2)}) copy-start(f32[1300]{0:T(1024)} %param.11) | copy-start | bytes 15604
  799.1 2.6 copy-start.3
  803.3 68.1 %copy-start.2 = (f32[1024,400]{0,1:T(8,128)S(1)}, f32[1024,400]{0,1:T(8,128)}, u32[]{:S(2)}) copy-start(f32[1024,400]{0,1:T(8,128)} %reduce-scatter.3.cloned.1.call-done) | copy-start | bytes 4915204
  (1 other events, 0.7 us)
Sparse Core Ops, SparseCore 0:
  250.8 61.3 reduce-scatter.2
  316.9 42.6 all-gather.1
  447.5 351.4 all-reduce.1
  801.5 67.7 reduce-scatter.4
where the time goes:
time: 882 us
  waiting for transfers between devices  795 us (90%)
  matrix products  34.9 us (4%)
  other arithmetic  19.5 us (2%)
  starting transfers between devices  16.4 us (2%)
  between operations  14 us (2%)
    ppermute x4, waiting for transfers between devices, passed_along(): lax.ppermute(value, axis, [(i, (i + by) % size) for i in range(size)])  421 us
    psum x1, waiting for transfers between devices, per_device(): relation_total = relation_total + lax.psum(relation_part, ('dom', 'rep'))  204 us
    reduce_scatter x2, waiting for transfers between devices, per_device(): lax.psum_scatter(own_part + block_back, 'rep', scatter_dimension=0, tiled...  127 us
    all_gather x1, waiting for transfers between devices, per_device(): lax.all_gather(own_rows.astype(jnp.bfloat16), 'rep', axis=0, tiled=True)  42.7 us
    dot_general x6, matrix products, spread_rows(): lax.dot_general(indicator, values, (((0,), (0,)), ((), ())), preferred_el...  23.6 us
  transfers between devices with their start and end apart: 8, of which 8 were waited for; matrix products, arithmetic and copies ran while one was open for 3% of the time, Pallas kernels for 0%

commit v1 on v0

v1 whole, which is shorter than its diff:
```python
import functools

import jax
import jax.numpy as jnp
from jax import lax
from jax.experimental import pallas as pl
from jax.experimental.pallas import tpu as pltpu
from jax.sharding import PartitionSpec as P

MESH = pl.DeviceIdType.MESH
F32, BF16, I32 = jnp.float32, jnp.bfloat16, jnp.int32

RATE = 0.2
EPS = 1e-06
W = 400
HALF = 200
WIDE = 512
ROWS = 4096
SHARE = 1024
GROUP = 256
RELS = 1300
SLOTS = 1536
FIRST = 1024
CHUNKS = 2

SRC, TGT, RID = 0, 2, 4


def mat(a, b):
    return jnp.dot(a, b, preferred_element_type=F32)


def iota(shape, dim):
    return lax.broadcasted_iota(I32, shape, dim)


def to_column(row):
    eye = iota((128, 128), 0) == iota((128, 128), 1)
    parts = [
        jnp.sum(jnp.where(eye, row[:, k : k + 128], jnp.zeros((), row.dtype)), axis=1, keepdims=True)
        for k in range(0, row.shape[1], 128)
    ]
    return jnp.concatenate(parts, axis=0)


def to_row(column):
    eye = iota((128, 128), 0) == iota((128, 128), 1)
    return jnp.sum(jnp.where(eye, column, 0.0), axis=0, keepdims=True)


def block_terms(src, rel, tgt, live):
    s_re, s_im = src[:, :HALF], src[:, HALF:]
    r_re, r_im = rel[:, :HALF], rel[:, HALF:]
    queries = jnp.concatenate([s_re * r_re - s_im * r_im, s_re * r_im + s_im * r_re], axis=1).astype(BF16)
    scores = lax.dot_general(queries, tgt, (((1,), (1,)), ((), ())), preferred_element_type=F32)
    row_id, col_id = iota((GROUP, GROUP), 0), iota((GROUP, GROUP), 1)
    terms = jnp.where(col_id < live, jnp.exp(scores), 0.0)
    probs = terms / jnp.sum(terms, axis=1, keepdims=True)
    coeffs = jnp.where(row_id < live, probs - jnp.where(row_id == col_id, 1.0, 0.0), 0.0)
    coeffs_b = coeffs.astype(BF16)
    d_queries = mat(coeffs_b, tgt)
    d_keys = mat(coeffs.T.astype(BF16), queries).astype(BF16)
    q_re, q_im = d_queries[:, :HALF], d_queries[:, HALF:]
    d_rel = jnp.concatenate([q_re * s_re + q_im * s_im, q_im * s_re - q_re * s_im], axis=1).astype(BF16)
    d_src = jnp.concatenate([q_re * r_re + q_im * r_im, q_im * r_re - q_re * r_im], axis=1).astype(BF16)
    return d_src, d_rel, d_keys


def adagrad(rows, state, grads):
    state = state + jnp.sum(grads * grads, axis=1, keepdims=True) * (1.0 / W)
    return rows - RATE * grads / (jnp.sqrt(state) + EPS), state


def summed(ids, slot_ids, values):
    return mat(jnp.where(ids == slot_ids, 1.0, 0.0).astype(BF16), values)


def kernel(
    tab_hbm, rtab_hbm, state_v, state_s, rstate_s, idx_s, idx_v, live_s,
    ent_hbm, est_ref, rel_hbm, rmean_ref,
    tab, rtab, idx_in, req_s, comb, slot0, slot1,
    rows_a, rows_b, src1, req1, st_src1, st_req1, rel0, rel1,
    out_rows, tgt_in, back, c0, c1, own, own_st,
    drel, hsum, hsend, cin, xin, qsum, qsend, zin, yin, rst, dall,
    local_sem, send_sem, recv_sem,
):
    dom, rep = lax.axis_index("dom"), lax.axis_index("rep")
    core, y_lo = lax.rem(rep, 2), lax.div(rep, 2)
    x, z, y_hi = lax.rem(dom, 4), lax.rem(lax.div(dom, 4), 8), lax.div(dom, 32)
    y = 2 * y_hi + y_lo
    plane = 32 * y_hi

    core_mate = (dom, rep + 1 - 2 * core)
    y_mate = (dom, lax.rem(rep + 2, 4))
    cross_mate = (dom, lax.rem(rep + 2, 4) + 1 - 2 * core)
    after = (lax.rem(dom + 1, 64), rep)
    before = (lax.rem(dom + 63, 64), rep)
    other = (lax.rem(dom + 32, 64), lax.rem(rep + 2, 4))
    opposite = (lax.rem(dom + 32, 64), rep)
    x_peers = [(plane + 4 * z + lax.rem(x + k, 4), rep) for k in range(1, 4)]
    z_peers = [(plane + 4 * lax.rem(z + k, 8) + x, rep) for k in range(1, 8)]

    count = [0]

    def send(src, dst, device):
        i = count[0]
        count[0] += 1
        return pltpu.make_async_remote_copy(
            src_ref=src, dst_ref=dst, send_sem=send_sem.at[i], recv_sem=recv_sem.at[i],
            device_id=device, device_id_type=MESH,
        )

    def start(copies):
        for copy in copies:
            copy.start()

    load_tab = pltpu.make_async_copy(tab_hbm, tab, local_sem.at[0])
    load_rtab = pltpu.make_async_copy(rtab_hbm, rtab, local_sem.at[1])
    load_tab.start()
    load_rtab.start()

    barrier = pltpu.get_barrier_semaphore()
    greeted = [core_mate, y_mate, cross_mate, after, before, other, opposite] + x_peers + z_peers
    for device in greeted:
        pl.semaphore_signal(barrier, inc=1, device_id=device, device_id_type=MESH)
    pl.semaphore_wait(barrier, len(greeted))

    ask0 = send(idx_v, idx_in.at[0], after)
    ask1 = send(idx_v, idx_in.at[1], other)
    start([ask0, ask1])

    def gather(dst, table, index_of, state=None):
        def eight(g, carry):
            base = pl.multiple_of(g * 8, 8)
            for k in range(8):
                i = index_of(base + k)
                dst[pl.ds(base + k, 1), :] = table[pl.ds(i, 1), :]
                if state is not None:
                    state[pl.ds(base + k, 1), :] = jnp.full((1, 128), state_s[i], F32)
            return carry

        lax.fori_loop(0, GROUP // 8, eight, 0)

    load_rtab.wait()
    gather(rel0, rtab, lambda j: idx_s[RID, j])
    ask0.wait_recv()
    fetch0 = pltpu.make_async_copy(idx_in.at[0], req_s.at[0], local_sem.at[2])
    fetch0.start()
    load_tab.wait()
    fetch0.wait()
    gather(rows_a, tab, lambda j: req_s[0, TGT, j])
    out_rows[0] = rows_a[...].astype(BF16)
    rows_out0 = send(out_rows.at[0], tgt_in.at[0], before)
    rows_out0.start()

    gather(rows_b, tab, lambda j: idx_s[SRC, j])
    ask1.wait_recv()
    fetch1 = pltpu.make_async_copy(idx_in.at[1], req_s.at[1], local_sem.at[3])
    fetch1.start()
    comb[rep, 0:2, :] = idx_v[SRC : SRC + 2, :]
    comb[rep, 2:3, :] = idx_in[0, TGT : TGT + 1, :]
    comb[rep, 3:4, :] = idx_in[1, TGT + 1 : TGT + 2, :]
    comb[rep, 4:8, :] = jnp.zeros((4, GROUP), I32)
    combs = [send(comb.at[rep], comb.at[rep], device) for device in (core_mate, y_mate, cross_mate)]
    start(combs)
    fetch1.wait()
    gather(src1, tab, lambda j: idx_s[SRC + 1, j], st_src1)
    gather(req1, tab, lambda j: req_s[1, TGT + 1, j], st_req1)
    gather(rel1, rtab, lambda j: idx_s[RID + 1, j])

    first_rel = jnp.where(core == 0, (x * 8 + z) * 32, FIRST + (z * 4 + x) * 16)
    for k in range(32):
        rst[k : k + 1, :] = jnp.full((1, 128), rstate_s[jnp.minimum(first_rel + k, RELS - 1)], F32)

    drel[...] = jnp.zeros(drel.shape, BF16)
    own_rows = pl.multiple_of(rep * SHARE, SHARE)
    for k in range(8):
        own_st[k * 128 : (k + 1) * 128, :] = to_column(state_v[pl.ds(rep * 8 + k, 1), :])

    def block_at(ref, holder, kind, piece):
        size = GROUP // CHUNKS
        return ref.at[pl.ds(pl.multiple_of((2 * holder + kind) * GROUP + piece * size, size), size), :]

    def share_in_rep(ref, kind, piece):
        mine = block_at(ref, rep, kind, piece)
        to_core, to_y = send(mine, mine, core_mate), send(mine, mine, y_mate)
        got = block_at(ref, lax.rem(rep + 2, 4), kind, piece)
        onward = send(got, got, core_mate)
        return to_core, to_y, onward

    def round_terms(t, src, rel, c_ref, to):
        d_src, d_rel, d_keys = block_terms(src, rel, tgt_in[t], live_s[t, 0])
        back[t] = d_keys
        drel[t * GROUP : (t + 1) * GROUP, 0:W] = d_rel
        c_ref[pl.ds(pl.multiple_of((2 * rep) * GROUP, GROUP), GROUP), :] = d_src
        size = GROUP // CHUNKS
        return [
            send(back.at[t, pl.ds(k * size, size), :], block_at(c_ref, to[1], 1, k), to) for k in range(CHUNKS)
        ]

    src0_f = rows_b[...].astype(BF16).astype(F32)
    rel0_f = rel0[...].astype(BF16).astype(F32)
    rows_out0.wait_recv()
    backs0 = round_terms(0, src0_f, rel0_f, c0, after)
    shares0 = [share_in_rep(c0, 0, k) for k in range(CHUNKS)] + [share_in_rep(c0, 1, k) for k in range(CHUNKS)]
    start(backs0)
    for k in range(CHUNKS):
        start(shares0[k][:2])
    for copy in combs:
        copy.wait_recv()
    for b in range(4):
        for kind in range(2):
            at = (2 * b + kind) * GROUP
            slot0[0:1, at : at + GROUP] = comb[b, 2 * kind : 2 * kind + 1, :]
            slot1[0:1, at : at + GROUP] = comb[b, 2 * kind + 1 : 2 * kind + 2, :]
    src1_ids = to_column(idx_v[SRC + 1 : SRC + 2, :])
    req1_ids = to_column(idx_in[1, TGT + 1 : TGT + 2, :])
    for k in range(CHUNKS):
        backs0[k].wait_recv()
        start(shares0[CHUNKS + k][:2])
        shares0[k][1].wait_recv()
        shares0[k][2].start()
    for k in range(CHUNKS):
        shares0[CHUNKS + k][1].wait_recv()
        shares0[CHUNKS + k][2].start()
    for group in shares0:
        group[0].wait_recv()
        group[2].wait_recv()

    def updated(rows, state, ids):
        grads = summed(ids, slot0[0:1, :], c0[...])
        return adagrad(rows[...], state[:, 0:1], grads)[0].astype(BF16)

    out_rows[1] = updated(req1, st_req1, req1_ids)
    rows_out1 = send(out_rows.at[1], tgt_in.at[1], other)
    rows_out1.start()
    src1_f = updated(src1, st_src1, src1_ids).astype(F32)
    rel1_f = rel1[...].astype(BF16).astype(F32)

    def relation_part(tile, t):
        ids = iota((GROUP, 1), 0) + tile * GROUP
        return summed(ids, idx_v[RID + t : RID + t + 1, :], drel[t * GROUP : (t + 1) * GROUP, :])

    for tile in range(SLOTS // GROUP):
        hsum[tile * GROUP : (tile + 1) * GROUP, :] = relation_part(tile, 0)

    def own_step(tile, rows, slots, c_ref):
        lo = tile * GROUP
        ids = iota((GROUP, 1), 0) + (rep * SHARE + lo)
        grads = summed(ids, slots[0:1, :], c_ref[...])
        new_rows, new_state = adagrad(rows, own_st[lo : lo + GROUP, :], grads)
        own[lo : lo + GROUP, :] = new_rows
        own_st[lo : lo + GROUP, :] = new_state

    for tile in range(SHARE // GROUP):
        own_step(tile, tab[pl.ds(own_rows + tile * GROUP, GROUP), :], slot0, c0)

    rows_out1.wait_recv()
    backs1 = round_terms(1, src1_f, rel1_f, c1, other)
    shares1 = [share_in_rep(c1, 0, k) for k in range(CHUNKS)] + [share_in_rep(c1, 1, k) for k in range(CHUNKS)]
    for tile in range(SLOTS // GROUP):
        rows = slice(tile * GROUP, (tile + 1) * GROUP)
        both = hsum[rows, :] + relation_part(tile, 1)
        hsum[rows, :] = both
        hsend[rows, :] = both.astype(BF16)

    on_0, on_1 = core == 0, core == 1

    def at(ref, lo, size):
        return ref.at[pl.ds(pl.multiple_of(lo, size), size), :]

    def f32_at(ref, lo, size):
        return ref[pl.ds(pl.multiple_of(lo, size), size), :].astype(F32)

    core_0 = send(hsend.at[pl.ds(FIRST, SLOTS - FIRST), :], cin.at[pl.ds(0, SLOTS - FIRST), :], core_mate)
    core_1 = send(hsend.at[pl.ds(0, FIRST), :], cin, core_mate)

    @pl.when(on_0)
    def _():
        core_0.start()

    @pl.when(on_1)
    def _():
        core_1.start()

    start(backs1)
    for k in range(CHUNKS):
        start(shares1[k][:2])

    wide_x = [
        send(at(hsend, lax.rem(x + k, 4) * 256, 256), xin.at[pl.ds((k - 1) * 256, 256), :], x_peers[k - 1])
        for k in range(1, 4)
    ]
    wide_z = [
        send(at(hsend, FIRST + lax.rem(z + k, 8) * 64, 64), xin.at[pl.ds((k - 1) * 64, 64), :], z_peers[k - 1])
        for k in range(1, 8)
    ]
    thin_z = [
        send(at(qsend, lax.rem(z + k, 8) * 32, 32), zin.at[pl.ds((k - 1) * 32, 32), :], z_peers[k - 1])
        for k in range(1, 8)
    ]
    thin_x = [
        send(at(qsend, lax.rem(x + k, 4) * 16, 16), zin.at[pl.ds((k - 1) * 16, 16), :], x_peers[k - 1])
        for k in range(1, 4)
    ]

    def spread(first, place, parts, size, copies):
        for k in range(1, parts):
            lo = lax.rem(place + k, parts) * size
            hsend[pl.ds(pl.multiple_of(first + lo, size), size), :] = (
                f32_at(hsum, first + lo, size) + f32_at(cin, lo, size)
            ).astype(BF16)
            copies[k - 1].start()
        lo = place * size
        qsum[0:size, :] = f32_at(hsum, first + lo, size) + f32_at(cin, lo, size)

    def collect(parts, size, copies, landing):
        total = qsum[0:size, :]
        for k in range(1, parts):
            copies[k - 1].wait_recv()
            total = total + landing[(k - 1) * size : k * size, :].astype(F32)
        return total

    @pl.when(on_0)
    def _():
        core_1.wait_recv()
        core_0.wait_send()
        spread(0, x, 4, 256, wide_x)

    @pl.when(on_1)
    def _():
        core_0.wait_recv()
        core_1.wait_send()
        spread(FIRST, z, 8, 64, wide_z)

    for k in range(CHUNKS):
        backs1[k].wait_recv()
        start(shares1[CHUNKS + k][:2])
        shares1[k][1].wait_recv()
        shares1[k][2].start()

    @pl.when(on_0)
    def _():
        total = collect(4, 256, wide_x, xin)
        qsum[...] = total
        qsend[...] = total.astype(BF16)
        start(thin_z)

    @pl.when(on_1)
    def _():
        total = collect(8, 64, wide_z, xin)
        qsum[0:64, :] = total
        qsend[0:64, :] = total.astype(BF16)
        start(thin_x)

    for k in range(CHUNKS):
        shares1[CHUNKS + k][1].wait_recv()
        shares1[CHUNKS + k][2].start()

    def last(place, parts, size, copies):
        total = f32_at(qsum, place * size, size)
        for k in range(1, parts):
            copies[k - 1].wait_recv()
            total = total + zin[(k - 1) * size : k * size, :].astype(F32)
        yin[y, 0:size, :] = total.astype(BF16)

    @pl.when(on_0)
    def _():
        last(z, 8, 32, thin_z)

    @pl.when(on_1)
    def _():
        last(x, 4, 16, thin_x)
        yin[y, 16:32, :] = jnp.zeros((16, WIDE), BF16)

    y_sends = [send(yin.at[y], yin.at[y], device) for device in (y_mate, opposite, other)]
    start(y_sends)
    for copy in y_sends:
        copy.wait_recv()

    total = yin[0].astype(F32) + yin[1].astype(F32) + yin[2].astype(F32) + yin[3].astype(F32)
    mean = jnp.sum(total * total, axis=1, keepdims=True) * (1.0 / W)
    delta = -RATE * total / (jnp.sqrt(rst[:, 0:1] + mean) + EPS)
    mean_hi = mean.astype(BF16).astype(F32)
    lane = iota((32, WIDE), 1)
    delta = jnp.where(lane == W, mean_hi, jnp.where(lane == W + 1, mean - mean_hi, delta)).astype(BF16)

    x_row, z_row = x * 256, FIRST + z * 64
    own_0 = at(dall, x_row + z * 32, 32)
    own_1 = at(dall, z_row + x * 16, 16)
    out_z = [send(own_0, own_0, device) for device in z_peers]
    out_x = [send(own_1, own_1, device) for device in x_peers]
    all_0, all_1 = at(dall, x_row, 256), at(dall, z_row, 64)
    out_x2 = [send(all_0, all_0, device) for device in x_peers]
    out_z2 = [send(all_1, all_1, device) for device in z_peers]
    half_0, half_1 = dall.at[pl.ds(0, FIRST), :], dall.at[pl.ds(FIRST, SLOTS - FIRST), :]
    swap_0, swap_1 = send(half_0, half_0, core_mate), send(half_1, half_1, core_mate)

    @pl.when(on_0)
    def _():
        own_0[...] = delta
        start(out_z)

    @pl.when(on_1)
    def _():
        own_1[...] = delta[0:16, :]
        start(out_x)

    for group in shares1:
        group[0].wait_recv()
        group[2].wait_recv()

    def own_tiles(tiles):
        for tile in tiles:
            lo = tile * GROUP
            own_step(tile, own[lo : lo + GROUP, :], slot1, c1)

    own_tiles((0, 1))

    @pl.when(on_0)
    def _():
        for copy in out_z:
            copy.wait_recv()
        start(out_x2)

    @pl.when(on_1)
    def _():
        for copy in out_x:
            copy.wait_recv()
        start(out_z2)

    own_tiles((2, 3))
    store_own = pltpu.make_async_copy(own, ent_hbm, local_sem.at[4])
    store_own.start()
    for k in range(8):
        est_ref[k : k + 1, :] = to_row(own_st[k * 128 : (k + 1) * 128, :])

    @pl.when(on_0)
    def _():
        for copy in out_x2:
            copy.wait_recv()
        swap_0.start()
        swap_1.wait_recv()

    @pl.when(on_1)
    def _():
        for copy in out_z2:
            copy.wait_recv()
        swap_1.start()
        swap_0.wait_recv()

    rtab[...] = rtab[...] + dall[0:RELS, 0:W].astype(F32)
    store_rel = pltpu.make_async_copy(rtab, rel_hbm, local_sem.at[5])
    store_rel.start()
    for k in range(SLOTS // 128):
        part = dall[k * 128 : (k + 1) * 128, 384:512].astype(F32)
        rmean_ref[k : k + 1, :] = to_row(part[:, 16:17] + part[:, 17:18])

    for copy in [ask0, ask1, rows_out0, rows_out1] + combs + backs0 + backs1 + y_sends:
        copy.wait_send()
    for group in shares0 + shares1:
        for copy in group:
            copy.wait_send()

    @pl.when(on_0)
    def _():
        for copy in wide_x + thin_z + out_z + out_x2 + [swap_0]:
            copy.wait_send()

    @pl.when(on_1)
    def _():
        for copy in wide_z + thin_x + out_x + out_z2 + [swap_1]:
            copy.wait_send()

    store_own.wait()
    store_rel.wait()
    assert count[0] <= SEMS, count[0]


SEMS = 96


def per_device(
    entity_table, entity_state, relation_table, relation_state, source_rows, target_rows, relation_ids, live_counts
):
    idx = jnp.concatenate(
        [source_rows[:, 0], target_rows[:, 0], relation_ids[:, 0], jnp.zeros((2, GROUP), I32)], axis=0
    )
    vmem, smem = pl.BlockSpec(memory_space=pltpu.VMEM), pl.BlockSpec(memory_space=pltpu.SMEM)
    anywhere = pl.BlockSpec(memory_space=pl.ANY)
    block_f = pltpu.VMEM((GROUP, W), F32)
    splat = pltpu.VMEM((GROUP, 128), F32)
    blocks_b = pltpu.VMEM((2, GROUP, W), BF16)
    contributions = pltpu.VMEM((8 * GROUP, W), BF16)
    own, own_state, new_relations, mean = pl.pallas_call(
        kernel,
        out_shape=(
            jax.ShapeDtypeStruct((SHARE, W), F32),
            jax.ShapeDtypeStruct((8, 128), F32),
            jax.ShapeDtypeStruct((RELS, W), F32),
            jax.ShapeDtypeStruct((SLOTS // 128, 128), F32),
        ),
        in_specs=[anywhere, anywhere, vmem, smem, smem, smem, vmem, smem],
        out_specs=(anywhere, vmem, anywhere, vmem),
        scratch_shapes=[
            pltpu.VMEM((ROWS, W), F32),
            pltpu.VMEM((RELS, W), F32),
            pltpu.VMEM((2, 8, GROUP), I32),
            pltpu.SMEM((2, 8, GROUP), I32),
            pltpu.VMEM((4, 8, GROUP), I32),
            pltpu.VMEM((8, 8 * GROUP), I32),
            pltpu.VMEM((8, 8 * GROUP), I32),
            block_f, block_f, block_f, block_f,
            splat, splat,
            block_f, block_f,
            blocks_b, blocks_b, blocks_b,
            contributions, contributions,
            pltpu.VMEM((SHARE, W), F32),
            pltpu.VMEM((SHARE, 1), F32),
            pltpu.VMEM((2 * GROUP, WIDE), BF16),
            pltpu.VMEM((SLOTS, WIDE), F32),
            pltpu.VMEM((SLOTS, WIDE), BF16),
            pltpu.VMEM((FIRST, WIDE), BF16),
            pltpu.VMEM((768, WIDE), BF16),
            pltpu.VMEM((256, WIDE), F32),
            pltpu.VMEM((256, WIDE), BF16),
            pltpu.VMEM((224, WIDE), BF16),
            pltpu.VMEM((4, 32, WIDE), BF16),
            pltpu.VMEM((32, 128), F32),
            pltpu.VMEM((SLOTS, WIDE), BF16),
            pltpu.SemaphoreType.DMA((6,)),
            pltpu.SemaphoreType.DMA((SEMS,)),
            pltpu.SemaphoreType.DMA((SEMS,)),
        ],
        compiler_params=pltpu.CompilerParams(
            collective_id=0, has_side_effects=True, vmem_limit_bytes=56 * 1024 * 1024
        ),
    )(
        entity_table, relation_table, entity_state.reshape(ROWS // 128, 128), entity_state, relation_state, idx, idx,
        live_counts[:, 0],
    )
    new_state = relation_state + mean.reshape(-1)[:RELS]
    return own, own_state.reshape(-1), new_relations, new_state


def solution(mesh):
    in_specs = (
        P("dom", None),
        P("dom"),
        P(),
        P(),
        P(None, "dom", "rep"),
        P(None, "dom", "rep"),
        P(None, "dom", "rep"),
        P(None, "dom", "rep"),
    )
    out_specs = (P(("dom", "rep"), None), P(("dom", "rep")), P(), P())
    return jax.shard_map(per_device, mesh=mesh, in_specs=in_specs, out_specs=out_specs, check_vma=False)
```

time: 882 us -> 124 us (0.14)
  waiting for transfers between devices: 795 us -> 0 us
  Pallas kernels: 0 us -> 101 us
  matrix products: 34.9 us -> 0 us
  other arithmetic: 19.5 us -> 1.27 us
  local copies, waits for them, and re-layouts: 2.15 us -> 20.2 us
  starting transfers between devices: 16.4 us -> 0 us
  between operations: 14 us -> 0.68 us
    ppermute x4 -> x0, waiting for transfers between devices: 421 us -> none  [passed_along(): lax.ppermute(value, axis, [(i, (i + by) % size) for i in range(size)])]
    psum x1 -> x0, waiting for transfers between devices: 204 us -> none  [per_device(): relation_total = relation_total + lax.psum(relation_part, ('dom', 'rep'))]
    reduce_scatter x2 -> x0, waiting for transfers between devices: 127 us -> none  [per_device(): lax.psum_scatter(own_part + block_back, 'rep', scatter_dimension=0, tiled...]
    pallas_call x0 -> x1, Pallas kernels: none -> 101 us  [per_device(): pl.pallas_call(kernel, out_shape=(jax.ShapeDtypeStruct((SHARE, W), F32),...]
    all_gather x1 -> x0, waiting for transfers between devices: 42.7 us -> none  [per_device(): lax.all_gather(own_rows.astype(jnp.bfloat16), 'rep', axis=0, tiled=True)]
    dot_general x16 -> x0, matrix products: 34.9 us -> none  [the longest x6 23.6 us: spread_rows(): lax.dot_general(indicator, values, (((0,), (0,)), ((), ())), preferred_el...]
    unnamed x34 -> x15, local copies, waits for them, and re-layouts: 0.94 us -> 18.9 us
    ppermute x4 -> x0, starting transfers between devices: 16.2 us -> none  [passed_along(): lax.ppermute(value, axis, [(i, (i + by) % size) for i in range(size)])]
  transfers between devices with their start and end apart: 8 -> 0, of which waited for: 8 -> 0; matrix products, arithmetic and copies ran while one was open for 3% -> 0% of each run, Pallas kernels for 0% -> 0%
where the time goes in v1:
time: 124 us
  Pallas kernels  101 us (81%)
  local copies, waits for them, and re-layouts  20.2 us (16%)
  other arithmetic  1.27 us (1%)
    pallas_call x1, Pallas kernels, per_device(): pl.pallas_call(kernel, out_shape=(jax.ShapeDtypeStruct((SHARE, W), F32),...  101 us
    unnamed x15, local copies, waits for them, and re-layouts  18.9 us

profile of v1, /device:TPU:1, one launch (start us, length us, event | category | flops | bytes accessed | tf_op | source)
XLA Modules:
  0.0 123.5 jit_solution(7334039125446620655)
XLA Ops:
  0.6 0.1 pad.3.clone
  0.7 1.3 %copy.14.live_s = s32[2,1]{1,0:T(2,128)} copy(s32[2,1]{0,1:T(1,128)} %bitcast.15) | data formatting | bytes 16 | tf_op jit(solution)/shard_map/squeeze | solution.py:540
  2.0 0.7 copy.23
  2.7 0.7 copy_bitcast_fusion
  3.4 0.7 add_add_fusion.idx_s.idx_v
  4.1 3.4 %copy.13.rtab_hbm = f32[1300,400]{1,0:T(8,128)} copy(f32[1300,400]{0,1:T(8,128)} %param.10) | data formatting | bytes 4160000 | tf_op args[2]
  7.4 8.5 %copy.12.tab_hbm = f32[4096,400]{1,0:T(8,128)} copy(f32[4096,400]{0,1:T(8,128)} %param.8) | data formatting | bytes 13107200 | tf_op args[0]
  16.0 101.3 %shard_map.111 = (f32[1024,400]{1,0:T(8,128)}, f32[8,128]{1,0:T(8,128)}, f32[1300,400]{1,0:T(8,128)}, f32[12,128]{1,0:T(8,128)}) custom-call(f32[4096,400]{1,0:T(8,128)} %copy.12.tab_hbm, f32[1300,400]{1,0:T(8,128)} %copy.13.rtab_hbm, f32[32,128]{1,0:T(8,128)} %bitcast.11, f32[4096]{0:T(1024)} %state_s.1, f32[1300]{0:T(1024)} %rstate_s.1, ...), custom_call_target="tpu_custom_call" | custom-call | tf_op jit(solution)/shard_map/pallas_call | solution.py:495
  117.3 0.0 copy-start.1
  117.3 0.0 copy-start.2
  117.3 0.0 copy-start
  117.4 2.9 %copy.15 = f32[1024,400]{0,1:T(8,128)} copy(f32[1024,400]{1,0:T(8,128)} %get-tuple-element.12) | data formatting | bytes 3276800
  120.3 0.0 copy-start.3
  120.3 0.0 copy-done.1
  120.3 0.0 copy-done.2
  120.3 0.6 slice_add_fusion
  120.9 0.0 copy-done
  120.9 2.1 %copy.16 = f32[1300,400]{0,1:T(8,128)} copy(f32[1300,400]{1,0:T(8,128)S(1)} %copy-done) | data formatting | bytes 4160000
  122.9 0.0 copy-done.3
  122.9 0.6 copy.25
  (1 shorter events, 0.0 us)
Async XLA Ops:
  117.3 2.9 %copy-start.1 = (f32[1300]{0:T(1024)S(1)}, f32[1300]{0:T(1024)}, u32[]{:S(2)}) copy-start(f32[1300]{0:T(1024)} %rstate_s.1) | copy-start | bytes 15604
  117.3 2.9 %copy-start.2 = (f32[12,128]{1,0:T(8,128)S(1)}, f32[12,128]{1,0:T(8,128)}, u32[]{:S(2)}) copy-start(f32[12,128]{1,0:T(8,128)} %get-tuple-element.11) | copy-start | bytes 18436
  117.3 3.5 %copy-start = (f32[1300,400]{1,0:T(8,128)S(1)}, f32[1300,400]{1,0:T(8,128)}, u32[]{:S(2)}) copy-start(f32[1300,400]{1,0:T(8,128)} %get-tuple-element.14) | copy-start | bytes 6240004
  120.3 2.7 %copy-start.3 = (f32[8,128]{1,0:T(8,128)S(1)}, f32[8,128]{1,0:T(8,128)}, u32[]{:S(2)}) copy-start(f32[8,128]{1,0:T(8,128)} %get-tuple-element.9) | copy-start | bytes 12292

commit v2 on v0

v2 whole, which is shorter than its diff:
```python
import jax
import jax.numpy as jnp
from jax import lax
from jax.experimental import pallas as pl
from jax.experimental.pallas import tpu as pltpu
from jax.sharding import PartitionSpec as P

MESH = pl.DeviceIdType.MESH
F32, BF16, I32 = jnp.float32, jnp.bfloat16, jnp.int32

RATE = 0.2
EPS = 1e-06
W = 400
HALF = 200
TALL = 416
WIDE = 512
ROWS = 4096
SHARE = 1024
GROUP = 256
RELS = 1300
FIRST = 1024
SECOND = 384
SLOTS = FIRST + SECOND
PER_0, PER_1 = 32, 48
PIECES = ((0, 208), (208, 192))
SEMS = 112


def mat(a, b):
    return jnp.dot(a, b, preferred_element_type=F32)


def iota(shape, dim):
    return lax.broadcasted_iota(I32, shape, dim)


def indicator(hit):
    return jnp.where(hit, 1.0, 0.0).astype(BF16)


def columns(rows):
    eye = indicator(iota((GROUP, GROUP), 0) == iota((GROUP, GROUP), 1))

    def turned(part):
        return lax.dot_general(
            eye, part.astype(F32).astype(BF16), (((1,), (1,)), ((), ())), preferred_element_type=F32
        )

    return turned(lax.shift_right_logical(rows, 8)) * 256.0 + turned(jnp.bitwise_and(rows, 255))


def adagrad(rows, state, grads):
    state = state + jnp.sum(grads * grads, axis=0, keepdims=True) * (1.0 / W)
    return rows - RATE * grads / (jnp.sqrt(state) + EPS), state


def kernel(
    tab_hbm, rtab_hbm, state_v, rstate_s, src_v, tgt_v, rid_v, live_s,
    ent_hbm, est_ref, rel_hbm, rmean_ref,
    tab, rtab, parts, rtab_b, st_parts, msg, idx_in, comb, cid,
    out_rows, tgt_in, back, c0, c1, gsum, own, own_st,
    h0, hsend, cin0, cin1, xin, qsum, hrow, zin, xex, yin, rst, drow, dout, dall,
    local_sem, send_sem, recv_sem,
):
    dom, rep = lax.axis_index("dom"), lax.axis_index("rep")
    core, y_lo = lax.rem(rep, 2), lax.div(rep, 2)
    x, z, y_hi = lax.rem(dom, 4), lax.rem(lax.div(dom, 4), 8), lax.div(dom, 32)
    y = 2 * y_hi + y_lo
    plane = 32 * y_hi
    on_0, on_1 = core == 0, core == 1

    core_rep, y_rep = rep + 1 - 2 * core, lax.rem(rep + 2, 4)
    core_mate, y_mate = (dom, core_rep), (dom, y_rep)
    cross_mate = (dom, y_rep + 1 - 2 * core)
    after = (lax.rem(dom + 1, 64), rep)
    before = (lax.rem(dom + 63, 64), rep)
    other = (lax.rem(dom + 32, 64), y_rep)
    opposite = (lax.rem(dom + 32, 64), rep)
    x_peers = [(plane + 4 * z + lax.rem(x + k, 4), rep) for k in range(1, 4)]
    z_peers = [(plane + 4 * lax.rem(z + k, 8) + x, rep) for k in range(1, 8)]

    count = [0]

    def send(src, dst, device):
        i = count[0]
        count[0] += 1
        assert i < SEMS
        return pltpu.make_async_remote_copy(
            src_ref=src, dst_ref=dst, send_sem=send_sem.at[i], recv_sem=recv_sem.at[i],
            device_id=device, device_id_type=MESH,
        )

    def start(copies):
        for copy in copies:
            copy.start()

    def lanes(ref, lo, size):
        return ref.at[:, pl.ds(pl.multiple_of(lo, 128), size)]

    def at_rows(ref, lo, size):
        return ref.at[pl.ds(pl.multiple_of(lo, 16), size), :]

    loads = [
        pltpu.make_async_copy(lanes(tab_hbm, k * 1024, 1024), lanes(tab, k * 1024, 1024), local_sem.at[k])
        for k in range(4)
    ]
    start(loads)
    load_rtab = pltpu.make_async_copy(rtab_hbm, rtab, local_sem.at[4])
    load_rtab.start()

    barrier = pltpu.get_barrier_semaphore()
    greeted = [core_mate, y_mate, cross_mate, after, before, other, opposite] + x_peers + z_peers
    for device in greeted:
        pl.semaphore_signal(barrier, inc=1, device_id=device, device_id_type=MESH)
    for t in range(2):
        msg[t : t + 1, :] = src_v[t]
        msg[2 + t : 3 + t, :] = tgt_v[t]
        msg[4 + t : 5 + t, :] = rid_v[t]
    msg[6:8, :] = jnp.zeros((2, GROUP), I32)
    pl.semaphore_wait(barrier, len(greeted))

    ask0 = send(msg, idx_in.at[0], after)
    ask1 = send(msg, idx_in.at[1], other)
    start([ask0, ask1])

    def lookup(table, ids):
        return mat(table, indicator(iota((table.shape[1], GROUP), 0) == ids))

    def high(k, carry):
        at = pl.ds(pl.multiple_of(k * 256, 256), 256)
        parts[0:W, at] = tab[:, at].astype(BF16)
        return carry

    for k in range(4):
        loads[k].wait()
        lax.fori_loop(4 * k, 4 * k + 4, high, 0)

    ask0.wait_recv()
    out_rows[0] = lookup(parts[0:W, :], idx_in[0, 2:3, :]).astype(BF16)
    rows_out0 = send(out_rows.at[0], tgt_in.at[0], before)
    rows_out0.start()
    ask1.wait_recv()

    comb[rep, 0:2, :] = msg[0:2, :]
    comb[rep, 2:3, :] = idx_in[0, 2:3, :]
    comb[rep, 3:4, :] = idx_in[1, 3:4, :]
    comb[rep, 4:8, :] = jnp.zeros((4, GROUP), I32)
    combs = [send(comb.at[rep], comb.at[rep], device) for device in (core_mate, y_mate, cross_mate)]
    start(combs)

    def product(a, b):
        return jnp.concatenate(
            [a[:HALF] * b[:HALF] - a[HALF:] * b[HALF:], a[:HALF] * b[HALF:] + a[HALF:] * b[:HALF]], axis=0
        )

    def conj_product(a, b):
        return jnp.concatenate(
            [a[:HALF] * b[:HALF] + a[HALF:] * b[HALF:], a[HALF:] * b[:HALF] - a[:HALF] * b[HALF:]], axis=0
        )

    def coefficients(queries_row, tgt, live):
        scores = mat(queries_row, tgt)
        row_id, col_id = iota((GROUP, GROUP), 0), iota((GROUP, GROUP), 1)
        terms = jnp.where(col_id < live, jnp.exp(scores), 0.0)
        probs = terms / jnp.sum(terms, axis=1, keepdims=True)
        return jnp.where(row_id < live, probs - jnp.where(row_id == col_id, 1.0, 0.0), 0.0)

    src0 = lookup(parts[0:W, :], msg[0:1, :])
    load_rtab.wait()
    rtab_b[...] = rtab[...].astype(BF16)
    rel0 = lookup(rtab_b[...], msg[4:5, :])
    queries0 = product(src0, rel0)
    queries0_row = queries0.T.astype(BF16)
    queries0 = queries0.astype(BF16)

    def low(k, carry):
        at = pl.ds(pl.multiple_of(k * 256, 256), 256)
        parts[W : 2 * W, at] = (tab[:, at] - parts[0:W, at].astype(F32)).astype(BF16)
        return carry

    lax.fori_loop(0, ROWS // 256, low, 0)
    st_parts[...] = jnp.zeros(st_parts.shape, F32)
    for k in range(ROWS // 128):
        whole = state_v[k : k + 1, :]
        top = whole.astype(BF16).astype(F32)
        mid = (whole - top).astype(BF16).astype(F32)
        st_parts[0:1, k * 128 : (k + 1) * 128] = top
        st_parts[1:2, k * 128 : (k + 1) * 128] = mid
        st_parts[2:3, k * 128 : (k + 1) * 128] = whole - top - mid
    parts[2 * W : 2 * W + 16, :] = st_parts[...].astype(BF16)

    def lookup_f32(ids):
        got = lookup(parts[...], ids)
        state = got[2 * W : 2 * W + 1] + got[2 * W + 1 : 2 * W + 2] + got[2 * W + 2 : 2 * W + 3]
        return got[0:W] + got[W : 2 * W], state

    req1_ids, src1_ids = idx_in[1, 3:4, :], msg[1:2, :]
    req1, req1_st = lookup_f32(req1_ids)
    src1, src1_st = lookup_f32(src1_ids)
    rel1 = lookup(rtab_b[...], msg[5:6, :])
    own_ids = columns(msg[...])
    for copy in combs:
        copy.wait_recv()
    for b in range(4):
        turned = columns(comb[b])
        for q in range(4):
            cid[q, b * GROUP : (b + 1) * GROUP, :] = turned[:, q : q + 1]

    first_rel = jnp.where(on_0, (x * 8 + z) * PER_0, FIRST + z * PER_1)
    for k in range(PER_1):
        rst[k : k + 1, :] = jnp.full((1, 128), rstate_s[jnp.minimum(first_rel + k, RELS - 1)], F32)
    hrow[...] = jnp.zeros(hrow.shape, F32)
    for k in range(8):
        own_st[0:1, k * 128 : (k + 1) * 128] = state_v[pl.ds(rep * 8 + k, 1), :]

    def block_at(ref, holder, kind, piece):
        lo, size = PIECES[piece]
        return ref.at[pl.ds(lo, size), pl.ds(pl.multiple_of(kind * 1024 + holder * GROUP, GROUP), GROUP)]

    def share_in_rep(ref, kind, piece):
        mine, got = block_at(ref, rep, kind, piece), block_at(ref, y_rep, kind, piece)
        return send(mine, mine, core_mate), send(mine, mine, y_mate), send(got, got, core_mate)

    def back_copies(t, ref, to):
        return [
            send(back.at[t, pl.ds(lo, size), :], block_at(ref, to[1], 1, k), to)
            for k, (lo, size) in enumerate(PIECES)
        ]

    def share_copies(ref):
        return [[share_in_rep(ref, kind, k) for k in range(len(PIECES))] for kind in range(2)]

    def mine_at(ref):
        return pl.ds(pl.multiple_of(rep * GROUP, GROUP), GROUP)

    rows_out0.wait_recv()
    backs0, shares0 = back_copies(0, c0, after), share_copies(c0)
    coeffs = coefficients(queries0_row, tgt_in[0], live_s[0])
    back[0] = mat(queries0, coeffs.astype(BF16)).astype(BF16)
    start(backs0)
    d_queries = mat(tgt_in[0], coeffs.T.astype(BF16))
    c0[:, mine_at(c0)] = conj_product(d_queries, rel0).astype(BF16)
    for group in shares0[0]:
        start(group[:2])
    d_rel0 = conj_product(d_queries, src0).astype(BF16)

    def relation_part(d_rel, rid, lo, size):
        return mat(d_rel, indicator(rid == (iota((1, size), 1) + lo).astype(F32)))

    for lo in range(0, SLOTS, 128):
        h0[:, lo : lo + 128] = relation_part(d_rel0, own_ids[:, 4:5], lo, 128)

    for k in range(len(PIECES)):
        backs0[k].wait_recv()
        start(shares0[1][k][:2])
        shares0[0][k][1].wait_recv()
        shares0[0][k][2].start()
    for group in shares0[0]:
        group[0].wait_recv()
        group[2].wait_recv()

    def summed(ref, kind, q, ids):
        return mat(ref[:, kind * 1024 : (kind + 1) * 1024], indicator(cid[q] == ids.astype(F32)))

    own_first = rep * SHARE

    def tile_ids(tile):
        return iota((1, GROUP), 1) + (own_first + tile * GROUP)

    gsum[:, 0:256] = summed(c0, 0, 0, req1_ids)
    gsum[:, 256:512] = summed(c0, 0, 0, src1_ids)
    for group in shares0[1]:
        group[1].wait_recv()
        group[2].start()
    for group in shares0[1]:
        group[0].wait_recv()
        group[2].wait_recv()

    grads = gsum[:, 0:256] + summed(c0, 1, 2, req1_ids)
    out_rows[1] = adagrad(req1, req1_st, grads)[0].astype(BF16)
    rows_out1 = send(out_rows.at[1], tgt_in.at[1], other)
    rows_out1.start()
    grads = gsum[:, 256:512] + summed(c0, 1, 2, src1_ids)
    src1 = adagrad(src1, src1_st, grads)[0].astype(BF16).astype(F32)
    queries1 = product(src1, rel1)
    queries1_row = queries1.T.astype(BF16)
    queries1 = queries1.astype(BF16)

    for tile in range(SHARE // GROUP):
        at = slice(tile * GROUP, (tile + 1) * GROUP)
        grads = summed(c0, 0, 0, tile_ids(tile)) + summed(c0, 1, 2, tile_ids(tile))
        rows = tab[:, pl.ds(pl.multiple_of(own_first + tile * GROUP, GROUP), GROUP)]
        own[:, at], own_st[0:1, at] = adagrad(rows, own_st[0:1, at], grads)

    rows_out1.wait_recv()
    backs1, shares1 = back_copies(1, c1, other), share_copies(c1)
    coeffs = coefficients(queries1_row, tgt_in[1], live_s[1])
    d_queries = mat(tgt_in[1], coeffs.T.astype(BF16))
    d_rel1 = conj_product(d_queries, src1).astype(BF16)

    def relation_sum(lo, size):
        at = pl.ds(pl.multiple_of(lo, 128), size)
        return h0[:, at] + relation_part(d_rel1, own_ids[:, 5:6], lo, size)

    order = [lax.rem(x + k, 4) * 256 for k in (1, 2, 3, 0)]
    to_core_0 = [send(lanes(hsend, lo, 256), lanes(cin0, lo, 256), core_mate) for lo in order]
    to_core_1 = send(lanes(hsend, FIRST, SECOND), cin1, core_mate)
    wide_x = [send(lanes(hsend, order[k], 256), xin.at[k], x_peers[k]) for k in range(3)]
    wide_z = [
        send(at_rows(drow, lax.rem(z + k, 8) * PER_1, PER_1), zin.at[k - 1], z_peers[k - 1])
        for k in range(1, 8)
    ]
    thin_z = [
        send(at_rows(drow, lax.rem(z + k, 8) * PER_0, PER_0), zin.at[k - 1, pl.ds(0, PER_0), :], z_peers[k - 1])
        for k in range(1, 8)
    ]
    thin_x = [send(xex.at[x], xex.at[x], device) for device in x_peers]

    @pl.when(on_1)
    def _():
        for k in range(4):
            hsend[:, pl.ds(pl.multiple_of(order[k], 256), 256)] = relation_sum(order[k], 256).astype(BF16)
            to_core_0[k].start()

    @pl.when(on_0)
    def _():
        hsend[:, FIRST:SLOTS] = relation_sum(FIRST, SECOND).astype(BF16)
        to_core_1.start()

    back[1] = mat(queries1, coeffs.astype(BF16)).astype(BF16)
    start(backs1)
    c1[:, mine_at(c1)] = conj_product(d_queries, rel1).astype(BF16)
    for group in shares1[0]:
        start(group[:2])

    @pl.when(on_0)
    def _():
        for k in range(4):
            mine = relation_sum(order[k], 256)
            to_core_0[k].wait_recv()
            at = pl.ds(pl.multiple_of(order[k], 256), 256)
            mine = mine + cin0[:, at].astype(F32)
            if k < 3:
                hsend[:, at] = mine.astype(BF16)
                wide_x[k].start()
            else:
                qsum[:, 0:256] = mine

    @pl.when(on_1)
    def _():
        mine = relation_sum(FIRST, SECOND)
        to_core_1.wait_recv()
        turned = (mine + cin1[...].astype(F32)).T
        hrow[0:SECOND, 0:W] = turned
        drow[...] = hrow[...].astype(BF16)
        start(wide_z)

    for k in range(len(PIECES)):
        backs1[k].wait_recv()
        start(shares1[1][k][:2])
        shares1[0][k][1].wait_recv()
        shares1[0][k][2].start()

    def collect(copies, size, place):
        total = hrow[pl.ds(pl.multiple_of(place * size, 16), size), :]
        for k in range(7):
            copies[k].wait_recv()
            total = total + zin[k, 0:size, :].astype(F32)
        return total

    @pl.when(on_0)
    def _():
        total = qsum[:, 0:256]
        for k in range(3):
            wide_x[k].wait_recv()
            total = total + xin[k].astype(F32)
        hrow[0:256, 0:W] = total.T
        drow[0:256, :] = hrow[0:256, :].astype(BF16)
        start(thin_z)

    @pl.when(on_1)
    def _():
        xex[x] = collect(wide_z, PER_1, z).astype(BF16)
        start(thin_x)

    for group in shares1[1]:
        group[1].wait_recv()
        group[2].start()

    @pl.when(on_0)
    def _():
        yin[y, 0:PER_0, :] = collect(thin_z, PER_0, z).astype(BF16)
        yin[y, PER_0:PER_1, :] = jnp.zeros((PER_1 - PER_0, WIDE), BF16)

    @pl.when(on_1)
    def _():
        for copy in thin_x:
            copy.wait_recv()
        total = xex[0].astype(F32) + xex[1].astype(F32) + xex[2].astype(F32) + xex[3].astype(F32)
        yin[y] = total.astype(BF16)

    y_sends = [send(yin.at[y], yin.at[y], device) for device in (y_mate, opposite, other)]
    start(y_sends)
    for copy in y_sends:
        copy.wait_recv()

    total = yin[0].astype(F32) + yin[1].astype(F32) + yin[2].astype(F32) + yin[3].astype(F32)
    mean = jnp.sum(total * total, axis=1, keepdims=True) * (1.0 / W)
    delta = -RATE * total / (jnp.sqrt(rst[:, 0:1] + mean) + EPS)
    mean_hi = mean.astype(BF16).astype(F32)
    lane = iota((PER_1, WIDE), 1)
    delta = jnp.where(lane == W, mean_hi, jnp.where(lane == W + 1, mean - mean_hi, delta)).astype(BF16)

    own_0, own_1 = at_rows(dout, z * PER_0, PER_0), at_rows(dout, z * PER_1, PER_1)
    out_z0 = [send(own_0, own_0, device) for device in z_peers]
    out_z1 = [send(own_1, own_1, device) for device in z_peers]
    chunk = lanes(dall, x * 256, 256)
    out_x = [send(chunk, chunk, device) for device in x_peers]
    swap_0 = [send(chunk, chunk, core_mate)]
    for k in range(1, 4):
        got = lanes(dall, lax.rem(x + 4 - k, 4) * 256, 256)
        swap_0.append(send(got, got, core_mate))
    half_1 = lanes(dall, FIRST, SECOND)
    swap_1 = send(half_1, half_1, core_mate)

    @pl.when(on_0)
    def _():
        own_0[...] = delta[0:PER_0, :]
        start(out_z0)

    @pl.when(on_1)
    def _():
        own_1[...] = delta
        start(out_z1)

    for kind in range(2):
        for group in shares1[kind]:
            group[0].wait_recv()
            group[2].wait_recv()

    def own_tiles(tiles):
        for tile in tiles:
            at = slice(tile * GROUP, (tile + 1) * GROUP)
            grads = summed(c1, 0, 1, tile_ids(tile)) + summed(c1, 1, 3, tile_ids(tile))
            own[:, at], own_st[0:1, at] = adagrad(own[:, at], own_st[0:1, at], grads)

    own_tiles((0,))

    @pl.when(on_0)
    def _():
        for copy in out_z0:
            copy.wait_recv()
        dall[:, pl.ds(pl.multiple_of(x * 256, 256), 256)] = dout[0:256, :].astype(F32).T[0:TALL].astype(BF16)
        start(out_x)
        swap_0[0].start()

    @pl.when(on_1)
    def _():
        for copy in out_z1:
            copy.wait_recv()
        dall[:, FIRST:SLOTS] = dout[...].astype(F32).T[0:TALL].astype(BF16)
        swap_1.start()

    own_tiles((1, 2, 3))
    store_own = pltpu.make_async_copy(own, ent_hbm, local_sem.at[5])
    store_own.start()
    for k in range(8):
        est_ref[k : k + 1, :] = own_st[0:1, k * 128 : (k + 1) * 128]

    @pl.when(on_0)
    def _():
        for k in range(3):
            out_x[k].wait_recv()
            swap_0[k + 1].start()
        swap_1.wait_recv()

    @pl.when(on_1)
    def _():
        for copy in swap_0:
            copy.wait_recv()

    rtab[...] = rtab[...] + dall[0:W, 0:RELS].astype(F32)
    store_rel = pltpu.make_async_copy(rtab, rel_hbm, local_sem.at[6])
    store_rel.start()
    tail = dall[W:TALL, :].astype(F32)
    mean_row = tail[0:1, :] + tail[1:2, :]
    for k in range(SLOTS // 128):
        rmean_ref[k : k + 1, :] = mean_row[:, k * 128 : (k + 1) * 128]

    for copy in [ask0, ask1, rows_out0, rows_out1] + combs + backs0 + backs1 + y_sends:
        copy.wait_send()
    for group in shares0[0] + shares0[1] + shares1[0] + shares1[1]:
        for copy in group:
            copy.wait_send()

    @pl.when(on_0)
    def _():
        for copy in [to_core_1] + wide_x + thin_z + out_z0 + out_x + swap_0:
            copy.wait_send()

    @pl.when(on_1)
    def _():
        for copy in to_core_0 + wide_z + thin_x + out_z1 + [swap_1]:
            copy.wait_send()

    store_own.wait()
    store_rel.wait()


def per_device(
    entity_table, entity_state, relation_table, relation_state, source_rows, target_rows, relation_ids, live_counts
):
    vmem, smem = pl.BlockSpec(memory_space=pltpu.VMEM), pl.BlockSpec(memory_space=pltpu.SMEM)
    anywhere = pl.BlockSpec(memory_space=pl.ANY)
    contributions = pltpu.VMEM((W, 8 * GROUP), BF16)
    blocks = pltpu.VMEM((2, W, GROUP), BF16)
    own, own_state, new_relations, mean = pl.pallas_call(
        kernel,
        out_shape=(
            jax.ShapeDtypeStruct((W, SHARE), F32),
            jax.ShapeDtypeStruct((8, 128), F32),
            jax.ShapeDtypeStruct((W, RELS), F32),
            jax.ShapeDtypeStruct((SLOTS // 128, 128), F32),
        ),
        in_specs=[anywhere, anywhere, vmem, smem, vmem, vmem, vmem, smem],
        out_specs=(anywhere, vmem, anywhere, vmem),
        scratch_shapes=[
            pltpu.VMEM((W, ROWS), F32),
            pltpu.VMEM((W, RELS), F32),
            pltpu.VMEM((2 * W + 16, ROWS), BF16),
            pltpu.VMEM((W, RELS), BF16),
            pltpu.VMEM((16, ROWS), F32),
            pltpu.VMEM((8, GROUP), I32),
            pltpu.VMEM((2, 8, GROUP), I32),
            pltpu.VMEM((4, 8, GROUP), I32),
            pltpu.VMEM((4, 4 * GROUP, 1), F32),
            blocks, blocks, blocks,
            contributions, contributions,
            pltpu.VMEM((W, 2 * GROUP), F32),
            pltpu.VMEM((W, SHARE), F32),
            pltpu.VMEM((8, SHARE), F32),
            pltpu.VMEM((W, SLOTS), F32),
            pltpu.VMEM((W, SLOTS), BF16),
            pltpu.VMEM((W, FIRST), BF16),
            pltpu.VMEM((W, SECOND), BF16),
            pltpu.VMEM((3, W, 256), BF16),
            pltpu.VMEM((W, 256), F32),
            pltpu.VMEM((SECOND, WIDE), F32),
            pltpu.VMEM((7, PER_1, WIDE), BF16),
            pltpu.VMEM((4, PER_1, WIDE), BF16),
            pltpu.VMEM((4, PER_1, WIDE), BF16),
            pltpu.VMEM((PER_1, 128), F32),
            pltpu.VMEM((SECOND, WIDE), BF16),
            pltpu.VMEM((SECOND, WIDE), BF16),
            pltpu.VMEM((TALL, SLOTS), BF16),
            pltpu.SemaphoreType.DMA((7,)),
            pltpu.SemaphoreType.DMA((SEMS,)),
            pltpu.SemaphoreType.DMA((SEMS,)),
        ],
        compiler_params=pltpu.CompilerParams(
            collective_id=0, has_side_effects=True, vmem_limit_bytes=60 * 1024 * 1024
        ),
    )(
        entity_table.T, relation_table.T, entity_state.reshape(ROWS // 128, 128), relation_state,
        source_rows, target_rows, relation_ids, live_counts.reshape(-1),
    )
    new_state = relation_state + mean.reshape(-1)[:RELS]
    return own.T, own_state.reshape(-1), new_relations.T, new_state


def solution(mesh):
    in_specs = (
        P("dom", None),
        P("dom"),
        P(),
        P(),
        P(None, "dom", "rep"),
        P(None, "dom", "rep"),
        P(None, "dom", "rep"),
        P(None, "dom", "rep"),
    )
    out_specs = (P(("dom", "rep"), None), P(("dom", "rep")), P(), P())
    return jax.shard_map(per_device, mesh=mesh, in_specs=in_specs, out_specs=out_specs, check_vma=False)
```

time: 882 us -> 99.4 us (0.11)
  waiting for transfers between devices: 795 us -> 0 us
  Pallas kernels: 0 us -> 92.3 us
  matrix products: 34.9 us -> 0 us
  other arithmetic: 19.5 us -> 1.45 us
  starting transfers between devices: 16.4 us -> 0 us
  between operations: 14 us -> 0.68 us
    ppermute x4 -> x0, waiting for transfers between devices: 421 us -> none  [passed_along(): lax.ppermute(value, axis, [(i, (i + by) % size) for i in range(size)])]
    psum x1 -> x0, waiting for transfers between devices: 204 us -> none  [per_device(): relation_total = relation_total + lax.psum(relation_part, ('dom', 'rep'))]
    reduce_scatter x2 -> x0, waiting for transfers between devices: 127 us -> none  [per_device(): lax.psum_scatter(own_part + block_back, 'rep', scatter_dimension=0, tiled...]
    pallas_call x0 -> x1, Pallas kernels: none -> 92.3 us  [per_device(): pl.pallas_call(kernel, out_shape=(jax.ShapeDtypeStruct((W, SHARE), F32),...]
    all_gather x1 -> x0, waiting for transfers between devices: 42.7 us -> none  [per_device(): lax.all_gather(own_rows.astype(jnp.bfloat16), 'rep', axis=0, tiled=True)]
    dot_general x16 -> x0, matrix products: 34.9 us -> none  [the longest x6 23.6 us: spread_rows(): lax.dot_general(indicator, values, (((0,), (0,)), ((), ())), preferred_el...]
    ppermute x4 -> x0, starting transfers between devices: 16.2 us -> none  [passed_along(): lax.ppermute(value, axis, [(i, (i + by) % size) for i in range(size)])]
  transfers between devices with their start and end apart: 8 -> 0, of which waited for: 8 -> 0; matrix products, arithmetic and copies ran while one was open for 3% -> 0% of each run, Pallas kernels for 0% -> 0%
where the time goes in v2:
time: 99.4 us; the launch traced here: 99.2 us
  Pallas kernels  92.3 us (93%)
  local copies, waits for them, and re-layouts  4.76 us (5%)
  other arithmetic  1.45 us (1%)
    pallas_call x1, Pallas kernels, per_device(): pl.pallas_call(kernel, out_shape=(jax.ShapeDtypeStruct((W, SHARE), F32),...  92.3 us
    unnamed x9, local copies, waits for them, and re-layouts  4.76 us

profile of v2, /device:TPU:1, one launch (start us, length us, event | category | flops | bytes accessed | tf_op | source)
XLA Modules:
  0.0 99.2 jit_solution(15676006653792674614)
XLA Ops:
  0.6 0.0 copy-start.1
  0.6 92.3 %shard_map.111 = (f32[400,1024]{1,0:T(8,128)}, f32[8,128]{1,0:T(8,128)}, f32[400,1300]{1,0:T(8,128)}, f32[11,128]{1,0:T(8,128)}) custom-call(f32[400,4096]{1,0:T(8,128)} %bitcast.8, f32[400,1300]{1,0:T(8,128)} %bitcast.9, f32[32,128]{1,0:T(8,128)} %bitcast.12, f32[1300]{0:T(1024)} %rstate_s.1, s32[2,1,256]{2,1,0:T(1,128)} %src_v.1, s32[2,1,256]{2,1,0:T(1,128)} %tgt_v.1, ...), custom_call_target="tpu_custom_call" | custom-call | tf_op jit(solution)/shard_map/pallas_call | solution.py:517
  93.0 0.0 copy-start.2
  93.0 0.0 copy-start
  93.0 0.0 copy-done.1
  93.0 1.4 %slice_add_fusion = f32[1300]{0:T(1024)} fusion(f32[1300]{0:T(1024)S(1)} %copy-done.1, f32[1408]{0:T(1024)} %bitcast.13), kind=kLoop, calls=%fused_computation | loop fusion | flops 1300 | bytes 15600 | tf_op jit(solution)/shard_map/add | solution.py:567
  94.4 2.8 %copy.15 = f32[1024,400]{0,1:T(8,128)} copy(f32[1024,400]{0,1:T(8,128)} %bitcast.11) | data formatting | bytes 3276800
  97.2 0.0 copy-done.2
  97.2 0.6 copy.16
  97.8 0.0 copy-done
  97.8 1.4 %copy.17 = f32[1300,400]{0,1:T(8,128)} copy(f32[1300,400]{0,1:T(8,128)S(1)} %bitcast.10) | data formatting | bytes 4160000
Async XLA Ops:
  0.6 92.3 %copy-start.1 = (f32[1300]{0:T(1024)S(1)}, f32[1300]{0:T(1024)}, u32[]{:S(2)}) copy-start(f32[1300]{0:T(1024)} %rstate_s.1) | copy-start | bytes 15604
  93.0 4.3 %copy-start.2 = (f32[8,128]{1,0:T(8,128)S(1)}, f32[8,128]{1,0:T(8,128)}, u32[]{:S(2)}) copy-start(f32[8,128]{1,0:T(8,128)} %get-tuple-element.9) | copy-start | bytes 12292
  93.0 4.8 %copy-start = (f32[400,1300]{1,0:T(8,128)S(1)}, f32[400,1300]{1,0:T(8,128)}, u32[]{:S(2)}) copy-start(f32[400,1300]{1,0:T(8,128)} %get-tuple-element.10) | copy-start | bytes 6240004

commit v3 on v2

v3 whole, which is shorter than its diff:
```python
import jax
import jax.numpy as jnp
from jax import lax
from jax.experimental import pallas as pl
from jax.experimental.pallas import tpu as pltpu
from jax.sharding import PartitionSpec as P

MESH = pl.DeviceIdType.MESH
F32, BF16, I32 = jnp.float32, jnp.bfloat16, jnp.int32

RATE = 0.2
EPS = 1e-06
W = 400
HALF = 200
TALL = 416
WIDE = 512
ROWS = 4096
SHARE = 1024
GROUP = 256
RELS = 1300
HALF_SLOTS = 768
SLOTS = 2 * HALF_SLOTS
FIRST_PART, SECOND_PART, THIRD_PART = 192, 48, 16
PIECES = ((0, 208), (208, 192))
SEMS = 112


def mat(a, b):
    return jnp.dot(a, b, preferred_element_type=F32)


def iota(shape, dim):
    return lax.broadcasted_iota(I32, shape, dim)


def indicator(hit):
    return jnp.where(hit, 1.0, 0.0).astype(BF16)


def columns(rows):
    eye = indicator(iota((GROUP, GROUP), 0) == iota((GROUP, GROUP), 1))

    def turned(part):
        return lax.dot_general(
            eye, part.astype(F32).astype(BF16), (((1,), (1,)), ((), ())), preferred_element_type=F32
        )

    return turned(lax.shift_right_logical(rows, 8)) * 256.0 + turned(jnp.bitwise_and(rows, 255))


def adagrad(rows, state, grads):
    state = state + jnp.sum(grads * grads, axis=0, keepdims=True) * (1.0 / W)
    return rows - RATE * grads / (jnp.sqrt(state) + EPS), state


def kernel(
    tab_hbm, rtab_hbm, state_v, rstate_s, src_v, tgt_v, rid_v, live_s,
    own, est_ref, delta_ref,
    tab, rtab, parts, rtab_b, st_parts, msg, idx_in, comb, cid,
    out_rows, rows_in, back, c0, c1, gsum, req1, src1, req1_st, src1_st, rel1, drel, own_st,
    h0, hsend, dmate, xin, qsum, qsend, sin, rsum, rsend, zin, rst, dall,
    local_sem, send_sem, recv_sem,
):
    dom, rep = lax.axis_index("dom"), lax.axis_index("rep")
    core, y_lo = lax.rem(rep, 2), lax.div(rep, 2)
    x, z, y_hi = lax.rem(dom, 4), lax.rem(lax.div(dom, 4), 8), lax.div(dom, 32)
    y = 2 * y_hi + y_lo
    plane = 32 * y_hi

    core_rep, y_rep = rep + 1 - 2 * core, lax.rem(rep + 2, 4)
    core_mate, y_mate = (dom, core_rep), (dom, y_rep)
    cross_mate = (dom, y_rep + 1 - 2 * core)
    after = (lax.rem(dom + 1, 64), rep)
    before = (lax.rem(dom + 63, 64), rep)
    before_y, after_y = (lax.rem(dom + 63, 64), y_rep), (lax.rem(dom + 1, 64), y_rep)
    other = (lax.rem(dom + 32, 64), y_rep)
    opposite = (lax.rem(dom + 32, 64), rep)
    x_peers = [(plane + 4 * z + lax.rem(x + k, 4), rep) for k in range(1, 4)]
    z_peers = [(plane + 4 * lax.rem(z + k, 8) + x, rep) for k in range(1, 8)]

    def beside(in_x, in_y):
        y_there = lax.rem(y + in_y, 4)
        return 32 * lax.div(y_there, 2) + 4 * z + lax.rem(x + in_x, 4), 2 * lax.rem(y_there, 2) + core

    first_peers = [beside((1 - core) * k, core * k) for k in range(1, 4)]
    second_peers = [beside(core * k, (1 - core) * k) for k in range(1, 4)]
    first, second = (1 - core) * x + core * y, core * x + (1 - core) * y
    mine_from = core * HALF_SLOTS

    def third(k):
        place = lax.rem(z + 4 * core + k + 8, 8)
        return lax.rem(place, 3) == 0, lax.div(place, 3)

    count = [0]

    def send(src, dst, device):
        i = count[0]
        count[0] += 1
        assert i < SEMS
        return pltpu.make_async_remote_copy(
            src_ref=src, dst_ref=dst, send_sem=send_sem.at[i], recv_sem=recv_sem.at[i],
            device_id=device, device_id_type=MESH,
        )

    def start(copies):
        for copy in copies:
            copy.start()

    def lanes(ref, lo, size):
        return ref.at[:, pl.ds(pl.multiple_of(lo, 128), size)]

    def at_rows(ref, lo, size):
        return ref.at[pl.ds(pl.multiple_of(lo, 16), size), :]

    loads = [
        pltpu.make_async_copy(lanes(tab_hbm, k * 1024, 1024), lanes(tab, k * 1024, 1024), local_sem.at[k])
        for k in range(4)
    ]
    start(loads)
    load_rtab = pltpu.make_async_copy(rtab_hbm, rtab, local_sem.at[4])
    load_rtab.start()

    barrier = pltpu.get_barrier_semaphore()
    greeted = [core_mate, y_mate, cross_mate, after, before, after_y, before_y, other, opposite] + x_peers + z_peers
    for device in greeted:
        pl.semaphore_signal(barrier, inc=1, device_id=device, device_id_type=MESH)
    for t in range(2):
        msg[t : t + 1, :] = src_v[t]
        msg[2 + t : 3 + t, :] = tgt_v[t]
        msg[4 + t : 5 + t, :] = rid_v[t]
    msg[6:8, :] = jnp.full((2, GROUP), live_s[0], I32)
    pl.semaphore_wait(barrier, len(greeted))

    ask0 = send(msg, idx_in.at[0], after)
    ask1 = send(msg, idx_in.at[1], other)
    start([ask0, ask1])

    def lookup(table, ids):
        return mat(table, indicator(iota((table.shape[1], GROUP), 0) == ids))

    def high(k, carry):
        at = pl.ds(pl.multiple_of(k * 256, 256), 256)
        parts[0:W, at] = tab[:, at].astype(BF16)
        return carry

    for k in range(4):
        loads[k].wait()
        lax.fori_loop(4 * k, 4 * k + 4, high, 0)

    out_rows[0] = lookup(parts[0:W, :], msg[0:1, :]).astype(BF16)
    rows_out0 = send(out_rows.at[0], rows_in.at[0], after)
    rows_out0.start()

    def product(a, b):
        return jnp.concatenate(
            [a[:HALF] * b[:HALF] - a[HALF:] * b[HALF:], a[:HALF] * b[HALF:] + a[HALF:] * b[:HALF]], axis=0
        )

    def conj_product(a, b):
        return jnp.concatenate(
            [a[:HALF] * b[:HALF] + a[HALF:] * b[HALF:], a[HALF:] * b[:HALF] - a[:HALF] * b[HALF:]], axis=0
        )

    def coefficients(queries_row, tgt, live):
        scores = mat(queries_row, tgt)
        row_id, col_id = iota((GROUP, GROUP), 0), iota((GROUP, GROUP), 1)
        terms = jnp.where(col_id < live, jnp.exp(scores), 0.0)
        probs = terms / jnp.sum(terms, axis=1, keepdims=True)
        return jnp.where(row_id < live, probs - jnp.where(row_id == col_id, 1.0, 0.0), 0.0)

    def block_at(ref, holder, kind, piece):
        lo, size = PIECES[piece]
        return ref.at[pl.ds(lo, size), pl.ds(pl.multiple_of(kind * 1024 + holder * GROUP, GROUP), GROUP)]

    def share_in_rep(ref, kind, piece):
        mine, got = block_at(ref, rep, kind, piece), block_at(ref, y_rep, kind, piece)
        return send(mine, mine, core_mate), send(mine, mine, y_mate), send(got, got, core_mate)

    def back_copies(t, ref, to, kind):
        return [
            send(back.at[t, pl.ds(lo, size), :], block_at(ref, to[1], kind, k), to)
            for k, (lo, size) in enumerate(PIECES)
        ]

    def share_copies(ref):
        return [[share_in_rep(ref, kind, k) for k in range(len(PIECES))] for kind in range(2)]

    def mine_at(kind):
        return pl.ds(pl.multiple_of(kind * 1024 + rep * GROUP, GROUP), GROUP)

    ask0.wait_recv()
    tgt0 = lookup(parts[0:W, :], idx_in[0, 2:3, :]).astype(BF16)
    load_rtab.wait()
    rtab_b[...] = rtab[...].astype(BF16)
    rel0 = lookup(rtab_b[...], idx_in[0, 4:5, :])
    backs0, shares0 = back_copies(0, c0, before, 0), share_copies(c0)[1]
    backs0_y = [
        send(back.at[0, pl.ds(lo, size), :], block_at(c0, rep, 0, k), before_y)
        for k, (lo, size) in enumerate(PIECES)
    ]
    pass_on = [
        [send(block_at(c0, holder, 0, k), block_at(c0, holder, 0, k), core_mate) for holder in (rep, y_rep)]
        for k in range(len(PIECES))
    ]
    rows_out0.wait_recv()
    src0 = rows_in[0].astype(F32)
    queries = product(src0, rel0)
    coeffs = coefficients(queries.T.astype(BF16), tgt0, idx_in[0, 6:7, :])
    d_queries = mat(tgt0, coeffs.T.astype(BF16))
    back[0] = conj_product(d_queries, rel0).astype(BF16)
    for k in range(len(PIECES)):
        backs0[k].start()
        backs0_y[k].start()
    c0[:, mine_at(1)] = mat(queries.astype(BF16), coeffs.astype(BF16)).astype(BF16)
    for group in shares0:
        start(group[:2])
    drel[...] = jnp.zeros(drel.shape, BF16)
    drel[0, :, 0:W] = conj_product(d_queries, src0).T.astype(BF16)
    drel_sends = [send(drel.at[t], dmate.at[t], core_mate) for t in range(2)]
    drel_sends[0].start()

    ask1.wait_recv()
    comb[rep, 0:2, :] = msg[0:2, :]
    comb[rep, 2:3, :] = idx_in[0, 2:3, :]
    comb[rep, 3:4, :] = idx_in[1, 3:4, :]
    comb[rep, 4:5, :] = idx_in[0, 4:5, :]
    comb[rep, 5:6, :] = msg[5:6, :]
    comb[rep, 6:8, :] = jnp.zeros((2, GROUP), I32)
    combs = [send(comb.at[rep], comb.at[rep], device) for device in (core_mate, y_mate, cross_mate)]
    start(combs)

    def low(k, carry):
        at = pl.ds(pl.multiple_of(k * 256, 256), 256)
        parts[W : 2 * W, at] = (tab[:, at] - parts[0:W, at].astype(F32)).astype(BF16)
        return carry

    lax.fori_loop(0, ROWS // 256, low, 0)
    st_parts[...] = jnp.zeros(st_parts.shape, F32)
    for k in range(ROWS // 128):
        whole = state_v[k : k + 1, :]
        top = whole.astype(BF16).astype(F32)
        mid = (whole - top).astype(BF16).astype(F32)
        st_parts[0:1, k * 128 : (k + 1) * 128] = top
        st_parts[1:2, k * 128 : (k + 1) * 128] = mid
        st_parts[2:3, k * 128 : (k + 1) * 128] = whole - top - mid
    parts[2 * W : 2 * W + 16, :] = st_parts[...].astype(BF16)

    def lookup_f32(ids, rows, state):
        got = lookup(parts[...], ids)
        state[0:1, :] = got[2 * W : 2 * W + 1] + got[2 * W + 1 : 2 * W + 2] + got[2 * W + 2 : 2 * W + 3]
        rows[...] = got[0:W] + got[W : 2 * W]

    req1_ids, src1_ids = idx_in[1, 3:4, :], msg[1:2, :]
    lookup_f32(req1_ids, req1, req1_st)

    for k in range(len(PIECES)):
        shares0[k][1].wait_recv()
        shares0[k][2].start()

    lookup_f32(src1_ids, src1, src1_st)
    for copy in combs:
        copy.wait_recv()
    for b in range(4):
        turned = columns(comb[b])
        for q in range(4):
            cid[q, b * GROUP : (b + 1) * GROUP, :] = turned[:, q : q + 1]
    for k in range(len(PIECES)):
        backs0[k].wait_recv()
        pass_on[k][0].start()
        backs0_y[k].wait_recv()
        pass_on[k][1].start()
    for group in shares0:
        group[0].wait_recv()
        group[2].wait_recv()

    def summed(ref, kind, q, ids):
        return mat(ref[:, kind * 1024 : (kind + 1) * 1024], indicator(cid[q] == ids.astype(F32)))

    own_first = rep * SHARE

    def tile_ids(tile):
        return iota((1, GROUP), 1) + (own_first + tile * GROUP)

    gsum[:, 0:256] = summed(c0, 1, 2, req1_ids)
    gsum[:, 256:512] = summed(c0, 1, 2, src1_ids)
    def relation_part(t, rows, rid, lo):
        ids = iota((FIRST_PART, 1), 0) + (mine_from + lo)
        return mat(indicator(ids == rid), rows[t])

    drel_sends[0].wait_recv()
    for lo in range(0, HALF_SLOTS, FIRST_PART):
        h0[lo : lo + FIRST_PART, :] = relation_part(0, drel, idx_in[0, 4:5, :], lo) + relation_part(
            0, dmate, comb[core_rep, 4:5, :], lo
        )
    rel1[...] = lookup(rtab_b[...], msg[5:6, :])

    for group in pass_on:
        for copy in group:
            copy.wait_recv()

    def updated(rows, state, at, ids):
        grads = gsum[:, at] + summed(c0, 0, 0, ids)
        return adagrad(rows[...], state[0:1, :], grads)[0].astype(BF16)

    out_rows[1] = updated(req1, req1_st, slice(0, 256), req1_ids)
    rows_out1 = send(out_rows.at[1], rows_in.at[1], other)
    rows_out1.start()
    src1_b = updated(src1, src1_st, slice(256, 512), src1_ids)
    src1[...] = src1_b.astype(F32)
    queries = product(src1[...], rel1[...])
    queries_row, queries_b = queries.T.astype(BF16), queries.astype(BF16)

    sums_third, my_third = third(0)
    second_row = pl.multiple_of(mine_from + first * FIRST_PART + second * SECOND_PART, 16)
    third_row = pl.multiple_of(second_row + my_third * THIRD_PART, 16)
    for k in range(THIRD_PART):
        rst[k : k + 1, :] = jnp.full((1, 128), rstate_s[jnp.minimum(third_row + k, RELS - 1)], F32)
    for k in range(8):
        own_st[0:1, k * 128 : (k + 1) * 128] = state_v[pl.ds(rep * 8 + k, 1), :]

    for tile in range(SHARE // GROUP):
        at = slice(tile * GROUP, (tile + 1) * GROUP)
        grads = summed(c0, 0, 0, tile_ids(tile)) + summed(c0, 1, 2, tile_ids(tile))
        rows = tab[:, pl.ds(pl.multiple_of(own_first + tile * GROUP, GROUP), GROUP)]
        own[:, at], own_st[0:1, at] = adagrad(rows, own_st[0:1, at], grads)

    rows_out1.wait_recv()
    backs1, shares1 = back_copies(1, c1, other, 1), share_copies(c1)
    coeffs = coefficients(queries_row, rows_in[1], live_s[1])
    d_queries = mat(rows_in[1], coeffs.T.astype(BF16))
    drel[1, :, 0:W] = conj_product(d_queries, src1[...]).T.astype(BF16)

    drel_sends[1].start()

    def quarter(ref, lo):
        return at_rows(ref, lo, FIRST_PART)

    my_lo = [lax.rem(first + k, 4) * FIRST_PART for k in (1, 2, 3, 0)]
    firsts = [send(quarter(hsend, my_lo[k]), xin.at[k], first_peers[k]) for k in range(3)]
    for lo in my_lo:
        quarter(h0, lo)[...] += relation_part(1, drel, msg[5:6, :], lo)
    drel_sends[1].wait_recv()
    for k in range(4):
        total = quarter(h0, my_lo[k])[...] + relation_part(1, dmate, comb[core_rep, 5:6, :], my_lo[k])
        if k < 3:
            quarter(hsend, my_lo[k])[...] = total.astype(BF16)
            firsts[k].start()
        else:
            qsum[...] = total

    back[1] = mat(queries_b, coeffs.astype(BF16)).astype(BF16)
    start(backs1)
    c1[:, mine_at(0)] = conj_product(d_queries, rel1[...]).astype(BF16)
    for group in shares1[0]:
        start(group[:2])

    for k in range(3):
        firsts[k].wait_recv()
        qsum[...] += xin[k].astype(F32)
    qsend[...] = qsum[...].astype(BF16)

    seconds = [
        send(at_rows(qsend, lax.rem(second + k, 4) * SECOND_PART, SECOND_PART), sin.at[k - 1], second_peers[k - 1])
        for k in range(1, 4)
    ]
    start(seconds)
    for k in range(len(PIECES)):
        backs1[k].wait_recv()
        start(shares1[1][k][:2])
    total = at_rows(qsum, second * SECOND_PART, SECOND_PART)[...]
    for k in range(3):
        seconds[k].wait_recv()
        total = total + sin[k].astype(F32)
    rsum[...] = total
    rsend[...] = total.astype(BF16)

    thirds = [
        send(at_rows(rsend, third(k)[1] * THIRD_PART, THIRD_PART), zin.at[k - 1], z_peers[k - 1])
        for k in range(1, 8)
    ]
    for k in range(1, 8):
        pl.when(third(k)[0])(thirds[k - 1].start)
    for k in range(len(PIECES)):
        shares1[0][k][1].wait_recv()
        shares1[0][k][2].start()

    third_rows = at_rows(dall, third_row, THIRD_PART)
    out_z = [send(third_rows, third_rows, device) for device in z_peers]

    @pl.when(sums_third)
    def _():
        total = at_rows(rsum, my_third * THIRD_PART, THIRD_PART)[...]
        for k in range(7):
            thirds[k].wait_recv()
            total = total + zin[k].astype(F32)
        mean = jnp.sum(total * total, axis=1, keepdims=True) * (1.0 / W)
        delta = -RATE * total / (jnp.sqrt(rst[:, 0:1] + mean) + EPS)
        mean_hi = mean.astype(BF16).astype(F32)
        lane = iota((THIRD_PART, WIDE), 1)
        delta = jnp.where(lane == W, mean_hi, jnp.where(lane == W + 1, mean - mean_hi, delta))
        third_rows[...] = delta.astype(BF16)
        start(out_z)

    for group in shares1[1]:
        group[1].wait_recv()
        group[2].start()
    for kind in range(2):
        for group in shares1[kind]:
            group[0].wait_recv()
            group[2].wait_recv()

    def own_tiles(tiles):
        for tile in tiles:
            at = slice(tile * GROUP, (tile + 1) * GROUP)
            grads = summed(c1, 0, 1, tile_ids(tile)) + summed(c1, 1, 3, tile_ids(tile))
            own[:, at], own_st[0:1, at] = adagrad(own[:, at], own_st[0:1, at], grads)

    own_tiles((0,))
    for k in range(1, 8):
        pl.when(third(-k)[0])(out_z[k - 1].wait_recv)
    second_rows = at_rows(dall, second_row, SECOND_PART)
    out_second = [send(second_rows, second_rows, device) for device in second_peers]
    start(out_second)
    own_tiles((1,))
    for copy in out_second:
        copy.wait_recv()
    first_rows = quarter(dall, mine_from + first * FIRST_PART)
    out_first = [send(first_rows, first_rows, device) for device in first_peers]
    start(out_first)
    swaps = [send(first_rows, first_rows, core_mate)]
    for k in range(1, 4):
        got = quarter(dall, mine_from + lax.rem(first + 4 - k, 4) * FIRST_PART)
        swaps.append(send(got, got, core_mate))
    swaps[0].start()
    own_tiles((2, 3))
    for k in range(8):
        est_ref[k : k + 1, :] = own_st[0:1, k * 128 : (k + 1) * 128]
    for k in range(3):
        out_first[k].wait_recv()
        swaps[k + 1].start()

    def turn(lo):
        lo = pl.multiple_of(lo, 128)
        delta_ref[:, pl.ds(lo, HALF_SLOTS)] = dall[pl.ds(lo, HALF_SLOTS), :].astype(F32).T[0:TALL].astype(BF16)

    turn(mine_from)
    for copy in swaps:
        copy.wait_recv()
    turn((1 - core) * HALF_SLOTS)

    for copy in [ask0, ask1, rows_out0, rows_out1] + combs + backs0 + backs0_y + backs1 + drel_sends:
        copy.wait_send()
    for group in shares0 + pass_on + shares1[0] + shares1[1]:
        for copy in group:
            copy.wait_send()
    for copy in firsts + seconds + out_second + out_first + swaps:
        copy.wait_send()
    for k in range(1, 8):
        pl.when(third(k)[0])(thirds[k - 1].wait_send)

    @pl.when(sums_third)
    def _():
        for copy in out_z:
            copy.wait_send()


OWN_PIECES = ((0, 104), (104, 104), (208, 96), (304, 96))


def finish(own, own_state, delta, rtab, rstate, ent_hbm, est_ref, rel_hbm, nstate, total, sem):
    def pieces(source, target, first):
        return [
            pltpu.make_async_copy(source.at[pl.ds(lo, size), :], target.at[pl.ds(lo, size), :], sem.at[first + k])
            for k, (lo, size) in enumerate(OWN_PIECES)
        ]

    stores, rel_stores = pieces(own, ent_hbm, 0), pieces(total, rel_hbm, 4)
    for store in stores:
        store.start()
    for k, (lo, size) in enumerate(OWN_PIECES):
        at = slice(lo, lo + size)
        total[at, :] = rtab[at, :] + delta[at, 0:RELS].astype(F32)
        rel_stores[k].start()
    est_ref[...] = own_state[...]
    tail = delta[W:TALL, :].astype(F32)
    mean = tail[0:1, :] + tail[1:2, :]
    nstate[...] = rstate[...] + mean.reshape(SLOTS)[:RELS]
    for store in stores + rel_stores:
        store.wait()


def per_device(
    entity_table, entity_state, relation_table, relation_state, source_rows, target_rows, relation_ids, live_counts
):
    vmem, smem = pl.BlockSpec(memory_space=pltpu.VMEM), pl.BlockSpec(memory_space=pltpu.SMEM)
    anywhere = pl.BlockSpec(memory_space=pl.ANY)
    contributions = pltpu.VMEM((W, 8 * GROUP), BF16)
    blocks = pltpu.VMEM((2, W, GROUP), BF16)
    block_f, state_row = pltpu.VMEM((W, GROUP), F32), pltpu.VMEM((8, GROUP), F32)
    relations = relation_table.T
    own, own_state, delta = pl.pallas_call(
        kernel,
        out_shape=(
            pltpu.VMEM((W, SHARE), F32),
            pltpu.VMEM((8, 128), F32),
            pltpu.VMEM((TALL, SLOTS), BF16),
        ),
        in_specs=[anywhere, anywhere, vmem, smem, vmem, vmem, vmem, smem],
        out_specs=(vmem, vmem, vmem),
        scratch_shapes=[
            pltpu.VMEM((W, ROWS), F32),
            pltpu.VMEM((W, RELS), F32),
            pltpu.VMEM((2 * W + 16, ROWS), BF16),
            pltpu.VMEM((W, RELS), BF16),
            pltpu.VMEM((16, ROWS), F32),
            pltpu.VMEM((8, GROUP), I32),
            pltpu.VMEM((2, 8, GROUP), I32),
            pltpu.VMEM((4, 8, GROUP), I32),
            pltpu.VMEM((4, 4 * GROUP, 1), F32),
            blocks, blocks, blocks,
            contributions, contributions,
            pltpu.VMEM((W, 2 * GROUP), F32),
            block_f, block_f, state_row, state_row, block_f,
            pltpu.VMEM((2, GROUP, WIDE), BF16),
            pltpu.VMEM((8, SHARE), F32),
            pltpu.VMEM((HALF_SLOTS, WIDE), F32),
            pltpu.VMEM((HALF_SLOTS, WIDE), BF16),
            pltpu.VMEM((2, GROUP, WIDE), BF16),
            pltpu.VMEM((3, FIRST_PART, WIDE), BF16),
            pltpu.VMEM((FIRST_PART, WIDE), F32),
            pltpu.VMEM((FIRST_PART, WIDE), BF16),
            pltpu.VMEM((3, SECOND_PART, WIDE), BF16),
            pltpu.VMEM((SECOND_PART, WIDE), F32),
            pltpu.VMEM((SECOND_PART, WIDE), BF16),
            pltpu.VMEM((7, THIRD_PART, WIDE), BF16),
            pltpu.VMEM((THIRD_PART, 128), F32),
            pltpu.VMEM((SLOTS, WIDE), BF16),
            pltpu.SemaphoreType.DMA((7,)),
            pltpu.SemaphoreType.DMA((SEMS,)),
            pltpu.SemaphoreType.DMA((SEMS,)),
        ],
        compiler_params=pltpu.CompilerParams(
            collective_id=0, has_side_effects=True, vmem_limit_bytes=58 * 1024 * 1024
        ),
    )(
        entity_table.T, relations, entity_state.reshape(ROWS // 128, 128), relation_state,
        source_rows, target_rows, relation_ids, live_counts.reshape(-1),
    )
    own, own_state, new_relations, new_state = pl.pallas_call(
        finish,
        out_shape=(
            jax.ShapeDtypeStruct((W, SHARE), F32),
            jax.ShapeDtypeStruct((8, 128), F32),
            jax.ShapeDtypeStruct((W, RELS), F32),
            jax.ShapeDtypeStruct((RELS,), F32),
        ),
        in_specs=[vmem, vmem, vmem, vmem, vmem],
        out_specs=(anywhere, vmem, anywhere, vmem),
        scratch_shapes=[
            pltpu.VMEM((W, RELS), F32),
            pltpu.SemaphoreType.DMA((8,)),
        ],
        compiler_params=pltpu.CompilerParams(vmem_limit_bytes=12 * 1024 * 1024),
    )(own, own_state, delta, relations, relation_state)
    return own.T, own_state.reshape(-1), new_relations.T, new_state


def solution(mesh):
    in_specs = (
        P("dom", None),
        P("dom"),
        P(),
        P(),
        P(None, "dom", "rep"),
        P(None, "dom", "rep"),
        P(None, "dom", "rep"),
        P(None, "dom", "rep"),
    )
    out_specs = (P(("dom", "rep"), None), P(("dom", "rep")), P(), P())
    return jax.shard_map(per_device, mesh=mesh, in_specs=in_specs, out_specs=out_specs, check_vma=False)
```

time: 99.4 us -> 89.7 us (0.902)
  local copies, waits for them, and re-layouts: 4.76 us -> 0.01 us
  Pallas kernels: 92.3 us -> 88.8 us
  other arithmetic: 1.45 us -> 0 us
    unnamed x9 -> x4, local copies, waits for them, and re-layouts: 4.76 us -> 0.01 us
    pallas_call x1 -> x2, Pallas kernels: 92.3 us -> 88.8 us  [the longest x1 86.2 us: per_device(): pl.pallas_call(kernel, out_shape=(pltpu.VMEM((W, SHARE), F32), pltpu.VMEM...]
    add x1 -> x0, other arithmetic: 1.45 us -> none  [per_device(): new_state = relation_state + mean.reshape(-1)[:RELS]]
where the time goes in v3:
time: 89.7 us; the launch traced here: 89.6 us
  Pallas kernels  88.8 us (99%)
    pallas_call x1, Pallas kernels, per_device(): pl.pallas_call(kernel, out_shape=(pltpu.VMEM((W, SHARE), F32), pltpu.VMEM...  86.2 us
    pallas_call x1, Pallas kernels, per_device(): pl.pallas_call(finish, out_shape=(jax.ShapeDtypeStruct((W, SHARE), F32),...  2.57 us

profile of v3, /device:TPU:1, one launch (start us, length us, event | category | flops | bytes accessed | tf_op | source)
XLA Modules:
  0.0 89.6 jit_solution(11303785215820641285)
XLA Ops:
  0.6 0.0 copy-start
  0.6 0.0 copy-start.1
  0.7 86.2 %shard_map.111 = (f32[400,1024]{1,0:T(8,128)S(1)}, f32[8,128]{1,0:T(8,128)S(1)}, bf16[416,1536]{1,0:T(8,128)(2,1)S(1)}) custom-call(f32[400,4096]{1,0:T(8,128)} %bitcast.9, f32[400,1300]{1,0:T(8,128)} %bitcast.7, f32[32,128]{1,0:T(8,128)} %bitcast.10, f32[1300]{0:T(1024)} %rstate.1, s32[2,1,256]{2,1,0:T(1,128)} %src_v.1, s32[2,1,256]{2,1,0:T(1,128)} %tgt_v.1, ...), custom_call_target="tpu_custom_call" | custom-call | tf_op jit(solution)/shard_map/pallas_call | solution.py:501
  86.9 0.0 copy-done
  86.9 0.0 copy-done.1
  86.9 2.6 %shard_map.112 = (f32[400,1024]{1,0:T(8,128)}, f32[8,128]{1,0:T(8,128)}, f32[400,1300]{1,0:T(8,128)}, f32[1300]{0:T(1024)}) custom-call(f32[400,1024]{1,0:T(8,128)S(1)} %get-tuple-element.11.own, f32[8,128]{1,0:T(8,128)S(1)} %get-tuple-element.12.own_state, bf16[416,1536]{1,0:T(8,128)(2,1)S(1)} %get-tuple-element.13.delta, f32[400,1300]{1,0:T(8,128)S(1)} %bitcast.8, ...), custom_call_target="tpu_custom_call" | custom-call | tf_op jit(solution)/shard_map/pallas_call | solution.py:549
Async XLA Ops:
  0.6 86.2 %copy-start = (f32[1300,400]{0,1:T(8,128)S(1)}, f32[1300,400]{0,1:T(8,128)}, u32[]{:S(2)}) copy-start(f32[1300,400]{0,1:T(8,128)} %param.10) | copy-start | bytes 6240004
  0.6 86.2 %copy-start.1 = (f32[1300]{0:T(1024)S(1)}, f32[1300]{0:T(1024)}, u32[]{:S(2)}) copy-start(f32[1300]{0:T(1024)} %rstate.1) | copy-start | bytes 15604

commit v4 on v3

--- a/solution.py
+++ b/solution.py
@@ -1,3 +1,5 @@
+import functools
+
 import jax
 import jax.numpy as jnp
 from jax import lax
@@ -20,9 +22,10 @@
 RELS = 1300
 HALF_SLOTS = 768
 SLOTS = 2 * HALF_SLOTS
-FIRST_PART, SECOND_PART, THIRD_PART = 192, 48, 16
+FIRST_PART, CHAIN, THIRD_PART = 192, 64, 16
+CHAINS = 3
 PIECES = ((0, 208), (208, 192))
-SEMS = 112
+SEMS = 128
 
 
 def mat(a, b):
@@ -54,9 +57,9 @@
 
 
 def kernel(
-    tab_hbm, rtab_hbm, state_v, rstate_s, src_v, tgt_v, rid_v, live_s,
-    own, est_ref, delta_ref,
-    tab, rtab, parts, rtab_b, st_parts, msg, idx_in, comb, cid,
+    tab_hbm, rtab_hbm, state_hbm, rstate_hbm, src_hbm, tgt_hbm, rid_hbm, live_hbm,
+    own, est_ref, rtab, mean_ref,
+    tab, parts, rtab_b, st_parts, state_v, rstate_s, src_v, tgt_v, rid_v, live_s, msg, idx_in, comb, cid,
     out_rows, rows_in, back, c0, c1, gsum, req1, src1, req1_st, src1_st, rel1, drel, own_st,
     h0, hsend, dmate, xin, qsum, qsend, sin, rsum, rsend, zin, rst, dall,
     local_sem, send_sem, recv_sem,
@@ -91,6 +94,9 @@
         place = lax.rem(z + 4 * core + k + 8, 8)
         return lax.rem(place, 3) == 0, lax.div(place, 3)
 
+    def holds(k, t):
+        return lax.rem(z + 4 * core + k + 8, 8) == 3 * t
+
     count = [0]
 
     def send(src, dst, device):
@@ -116,14 +122,25 @@
         pltpu.make_async_copy(lanes(tab_hbm, k * 1024, 1024), lanes(tab, k * 1024, 1024), local_sem.at[k])
         for k in range(4)
     ]
+    smalls = [
+        pltpu.make_async_copy(source, target, local_sem.at[5 + k])
+        for k, (source, target) in enumerate(
+            (
+                (src_hbm, src_v), (tgt_hbm, tgt_v), (rid_hbm, rid_v), (live_hbm, live_s),
+                (state_hbm, state_v), (rstate_hbm, rstate_s),
+            )
+        )
+    ]
+    start(smalls)
     start(loads)
     load_rtab = pltpu.make_async_copy(rtab_hbm, rtab, local_sem.at[4])
-    load_rtab.start()
 
     barrier = pltpu.get_barrier_semaphore()
     greeted = [core_mate, y_mate, cross_mate, after, before, after_y, before_y, other, opposite] + x_peers + z_peers
     for device in greeted:
         pl.semaphore_signal(barrier, inc=1, device_id=device, device_id_type=MESH)
+    for copy in smalls:
+        copy.wait()
     for t in range(2):
         msg[t : t + 1, :] = src_v[t]
         msg[2 + t : 3 + t, :] = tgt_v[t]
@@ -138,6 +155,26 @@
     def lookup(table, ids):
         return mat(table, indicator(iota((table.shape[1], GROUP), 0) == ids))
 
+    st_parts[...] = jnp.zeros(st_parts.shape, F32)
+    for k in range(ROWS // 128):
+        whole = state_v[k : k + 1, :]
+        top = whole.astype(BF16).astype(F32)
+        mid = (whole - top).astype(BF16).astype(F32)
+        st_parts[0:1, k * 128 : (k + 1) * 128] = top
+        st_parts[1:2, k * 128 : (k + 1) * 128] = mid
+        st_parts[2:3, k * 128 : (k + 1) * 128] = whole - top - mid
+    parts[W : W + 16, :] = st_parts[...].astype(BF16)
+
+    sums_third, my_third = third(0)
+    first_row = mine_from + first * FIRST_PART
+    third_row = pl.multiple_of(first_row + my_third * CHAIN + second * THIRD_PART, 16)
+    for k in range(THIRD_PART):
+        rst[k : k + 1, :] = jnp.full((1, 128), rstate_s[jnp.minimum(third_row + k, RELS - 1)], F32)
+    for k in range(8):
+        own_st[0:1, k * 128 : (k + 1) * 128] = state_v[pl.ds(rep * 8 + k, 1), :]
+
+    drel[...] = jnp.zeros(drel.shape, BF16)
+
     def high(k, carry):
         at = pl.ds(pl.multiple_of(k * 256, 256), 256)
         parts[0:W, at] = tab[:, at].astype(BF16)
@@ -146,6 +183,7 @@
     for k in range(4):
         loads[k].wait()
         lax.fori_loop(4 * k, 4 * k + 4, high, 0)
+    load_rtab.start()
 
     out_rows[0] = lookup(parts[0:W, :], msg[0:1, :]).astype(BF16)
     rows_out0 = send(out_rows.at[0], rows_in.at[0], after)
@@ -189,10 +227,29 @@
         return pl.ds(pl.multiple_of(kind * 1024 + rep * GROUP, GROUP), GROUP)
 
     ask0.wait_recv()
+    ask1.wait_recv()
+    comb[rep, 0:2, :] = msg[0:2, :]
+    comb[rep, 2:3, :] = idx_in[0, 2:3, :]
+    comb[rep, 3:4, :] = idx_in[1, 3:4, :]
+    comb[rep, 4:5, :] = idx_in[0, 4:5, :]
+    comb[rep, 5:6, :] = msg[5:6, :]
+    comb[rep, 6:8, :] = jnp.zeros((2, GROUP), I32)
+    combs = [send(comb.at[rep], comb.at[rep], device) for device in (core_mate, y_mate, cross_mate)]
+    start(combs)
+
     tgt0 = lookup(parts[0:W, :], idx_in[0, 2:3, :]).astype(BF16)
     load_rtab.wait()
     rtab_b[...] = rtab[...].astype(BF16)
     rel0 = lookup(rtab_b[...], idx_in[0, 4:5, :])
+
+    def lookup_all(ids, rows, state):
+        got = lookup(parts[...], ids)
+        state[0:1, :] = got[W : W + 1] + got[W + 1 : W + 2] + got[W + 2 : W + 3]
+        rows[...] = got[0:W]
+
+    req1_ids, src1_ids = idx_in[1, 3:4, :], msg[1:2, :]
+    lookup_all(req1_ids, req1, req1_st)
+
     backs0, shares0 = back_copies(0, c0, before, 0), share_copies(c0)[1]
     backs0_y = [
         send(back.at[0, pl.ds(lo, size), :], block_at(c0, rep, 0, k), before_y)
@@ -214,50 +271,11 @@
     c0[:, mine_at(1)] = mat(queries.astype(BF16), coeffs.astype(BF16)).astype(BF16)
     for group in shares0:
         start(group[:2])
-    drel[...] = jnp.zeros(drel.shape, BF16)
     drel[0, :, 0:W] = conj_product(d_queries, src0).T.astype(BF16)
     drel_sends = [send(drel.at[t], dmate.at[t], core_mate) for t in range(2)]
     drel_sends[0].start()
 
-    ask1.wait_recv()
-    comb[rep, 0:2, :] = msg[0:2, :]
-    comb[rep, 2:3, :] = idx_in[0, 2:3, :]
-    comb[rep, 3:4, :] = idx_in[1, 3:4, :]
-    comb[rep, 4:5, :] = idx_in[0, 4:5, :]
-    comb[rep, 5:6, :] = msg[5:6, :]
-    comb[rep, 6:8, :] = jnp.zeros((2, GROUP), I32)
-    combs = [send(comb.at[rep], comb.at[rep], device) for device in (core_mate, y_mate, cross_mate)]
-    start(combs)
-
-    def low(k, carry):
-        at = pl.ds(pl.multiple_of(k * 256, 256), 256)
-        parts[W : 2 * W, at] = (tab[:, at] - parts[0:W, at].astype(F32)).astype(BF16)
-        return carry
-
-    lax.fori_loop(0, ROWS // 256, low, 0)
-    st_parts[...] = jnp.zeros(st_parts.shape, F32)
-    for k in range(ROWS // 128):
-        whole = state_v[k : k + 1, :]
-        top = whole.astype(BF16).astype(F32)
-        mid = (whole - top).astype(BF16).astype(F32)
-        st_parts[0:1, k * 128 : (k + 1) * 128] = top
-        st_parts[1:2, k * 128 : (k + 1) * 128] = mid
-        st_parts[2:3, k * 128 : (k + 1) * 128] = whole - top - mid
-    parts[2 * W : 2 * W + 16, :] = st_parts[...].astype(BF16)
-
-    def lookup_f32(ids, rows, state):
-        got = lookup(parts[...], ids)
-        state[0:1, :] = got[2 * W : 2 * W + 1] + got[2 * W + 1 : 2 * W + 2] + got[2 * W + 2 : 2 * W + 3]
-        rows[...] = got[0:W] + got[W : 2 * W]
-
-    req1_ids, src1_ids = idx_in[1, 3:4, :], msg[1:2, :]
-    lookup_f32(req1_ids, req1, req1_st)
-
-    for k in range(len(PIECES)):
-        shares0[k][1].wait_recv()
-        shares0[k][2].start()
-
-    lookup_f32(src1_ids, src1, src1_st)
+    lookup_all(src1_ids, src1, src1_st)
     for copy in combs:
         copy.wait_recv()
     for b in range(4):
@@ -265,10 +283,9 @@
         for q in range(4):
             cid[q, b * GROUP : (b + 1) * GROUP, :] = turned[:, q : q + 1]
     for k in range(len(PIECES)):
-        backs0[k].wait_recv()
-        pass_on[k][0].start()
-        backs0_y[k].wait_recv()
-        pass_on[k][1].start()
+        shares0[k][1].wait_recv()
+        shares0[k][2].start()
+
     for group in shares0:
         group[0].wait_recv()
         group[2].wait_recv()
@@ -283,6 +300,7 @@
 
     gsum[:, 0:256] = summed(c0, 1, 2, req1_ids)
     gsum[:, 256:512] = summed(c0, 1, 2, src1_ids)
+
     def relation_part(t, rows, rid, lo):
         ids = iota((FIRST_PART, 1), 0) + (mine_from + lo)
         return mat(indicator(ids == rid), rows[t])
@@ -293,6 +311,11 @@
             0, dmate, comb[core_rep, 4:5, :], lo
         )
     rel1[...] = lookup(rtab_b[...], msg[5:6, :])
+    for k in range(len(PIECES)):
+        backs0[k].wait_recv()
+        pass_on[k][0].start()
+        backs0_y[k].wait_recv()
+        pass_on[k][1].start()
 
     for group in pass_on:
         for copy in group:
@@ -310,14 +333,6 @@
     queries = product(src1[...], rel1[...])
     queries_row, queries_b = queries.T.astype(BF16), queries.astype(BF16)
 
-    sums_third, my_third = third(0)
-    second_row = pl.multiple_of(mine_from + first * FIRST_PART + second * SECOND_PART, 16)
-    third_row = pl.multiple_of(second_row + my_third * THIRD_PART, 16)
-    for k in range(THIRD_PART):
-        rst[k : k + 1, :] = jnp.full((1, 128), rstate_s[jnp.minimum(third_row + k, RELS - 1)], F32)
-    for k in range(8):
-        own_st[0:1, k * 128 : (k + 1) * 128] = state_v[pl.ds(rep * 8 + k, 1), :]
-
     for tile in range(SHARE // GROUP):
         at = slice(tile * GROUP, (tile + 1) * GROUP)
         grads = summed(c0, 0, 0, tile_ids(tile)) + summed(c0, 1, 2, tile_ids(tile))
@@ -336,7 +351,14 @@
         return at_rows(ref, lo, FIRST_PART)
 
     my_lo = [lax.rem(first + k, 4) * FIRST_PART for k in (1, 2, 3, 0)]
-    firsts = [send(quarter(hsend, my_lo[k]), xin.at[k], first_peers[k]) for k in range(3)]
+    chains = range(CHAINS)
+    firsts = [
+        [
+            send(at_rows(hsend, my_lo[k] + t * CHAIN, CHAIN), xin.at[k, pl.ds(t * CHAIN, CHAIN), :], first_peers[k])
+            for k in range(3)
+        ]
+        for t in chains
+    ]
     for lo in my_lo:
         quarter(h0, lo)[...] += relation_part(1, drel, msg[5:6, :], lo)
     drel_sends[1].wait_recv()
@@ -344,9 +366,10 @@
         total = quarter(h0, my_lo[k])[...] + relation_part(1, dmate, comb[core_rep, 5:6, :], my_lo[k])
         if k < 3:
             quarter(hsend, my_lo[k])[...] = total.astype(BF16)
-            firsts[k].start()
+            firsts[0][k].start()
         else:
             qsum[...] = total
+    start(firsts[1] + firsts[2])
 
     back[1] = mat(queries_b, coeffs.astype(BF16)).astype(BF16)
     start(backs1)
@@ -354,33 +377,45 @@
     for group in shares1[0]:
         start(group[:2])
 
-    for k in range(3):
-        firsts[k].wait_recv()
-        qsum[...] += xin[k].astype(F32)
-    qsend[...] = qsum[...].astype(BF16)
-
     seconds = [
-        send(at_rows(qsend, lax.rem(second + k, 4) * SECOND_PART, SECOND_PART), sin.at[k - 1], second_peers[k - 1])
-        for k in range(1, 4)
-    ]
-    start(seconds)
+        [
+            send(
+                at_rows(qsend, t * CHAIN + lax.rem(second + k, 4) * THIRD_PART, THIRD_PART),
+                sin.at[k - 1, pl.ds(t * THIRD_PART, THIRD_PART), :],
+                second_peers[k - 1],
+            )
+            for k in range(1, 4)
+        ]
+        for t in chains
+    ]
+    for t in chains:
+        at = slice(t * CHAIN, (t + 1) * CHAIN)
+        total = qsum[at, :]
+        for k in range(3):
+            firsts[t][k].wait_recv()
+            total = total + xin[k, at, :].astype(F32)
+        qsum[at, :] = total
+        qsend[at, :] = total.astype(BF16)
+        start(seconds[t])
+
+    thirds = [
+        send(at_rows(rsend, third(k)[1] * THIRD_PART, THIRD_PART), zin.at[k - 1], z_peers[k - 1])
+        for k in range(1, 8)
+    ]
+    for t in chains:
+        at = slice(t * THIRD_PART, (t + 1) * THIRD_PART)
+        total = at_rows(qsum, t * CHAIN + second * THIRD_PART, THIRD_PART)[...]
+        for k in range(3):
+            seconds[t][k].wait_recv()
+            total = total + sin[k, at, :].astype(F32)
+        rsum[at, :] = total
+        rsend[at, :] = total.astype(BF16)
+        for k in range(1, 8):
+            pl.when(holds(k, t))(thirds[k - 1].start)
+
     for k in range(len(PIECES)):
         backs1[k].wait_recv()
         start(shares1[1][k][:2])
-    total = at_rows(qsum, second * SECOND_PART, SECOND_PART)[...]
-    for k in range(3):
-        seconds[k].wait_recv()
-        total = total + sin[k].astype(F32)
-    rsum[...] = total
-    rsend[...] = total.astype(BF16)
-
-    thirds = [
-        send(at_rows(rsend, third(k)[1] * THIRD_PART, THIRD_PART), zin.at[k - 1], z_peers[k - 1])
-        for k in range(1, 8)
-    ]
-    for k in range(1, 8):
-        pl.when(third(k)[0])(thirds[k - 1].start)
-    for k in range(len(PIECES)):
         shares1[0][k][1].wait_recv()
         shares1[0][k][2].start()
 
@@ -416,45 +451,53 @@
             own[:, at], own_st[0:1, at] = adagrad(own[:, at], own_st[0:1, at], grads)
 
     own_tiles((0,))
-    for k in range(1, 8):
-        pl.when(third(-k)[0])(out_z[k - 1].wait_recv)
-    second_rows = at_rows(dall, second_row, SECOND_PART)
-    out_second = [send(second_rows, second_rows, device) for device in second_peers]
-    start(out_second)
+    out_second, out_first, swaps = [], [], []
+    for t in chains:
+        for k in range(1, 8):
+            pl.when(holds(-k, t))(out_z[k - 1].wait_recv)
+        rows = at_rows(dall, first_row + t * CHAIN + second * THIRD_PART, THIRD_PART)
+        out_second.append([send(rows, rows, device) for device in second_peers])
+        start(out_second[t])
     own_tiles((1,))
-    for copy in out_second:
-        copy.wait_recv()
-    first_rows = quarter(dall, mine_from + first * FIRST_PART)
-    out_first = [send(first_rows, first_rows, device) for device in first_peers]
-    start(out_first)
-    swaps = [send(first_rows, first_rows, core_mate)]
-    for k in range(1, 4):
-        got = quarter(dall, mine_from + lax.rem(first + 4 - k, 4) * FIRST_PART)
-        swaps.append(send(got, got, core_mate))
-    swaps[0].start()
+    for t in chains:
+        for copy in out_second[t]:
+            copy.wait_recv()
+        rows = at_rows(dall, first_row + t * CHAIN, CHAIN)
+        out_first.append([send(rows, rows, device) for device in first_peers])
+        start(out_first[t])
+        swaps.append(send(rows, rows, core_mate))
+        swaps[t].start()
     own_tiles((2, 3))
     for k in range(8):
         est_ref[k : k + 1, :] = own_st[0:1, k * 128 : (k + 1) * 128]
-    for k in range(3):
-        out_first[k].wait_recv()
-        swaps[k + 1].start()
-
-    def turn(lo):
-        lo = pl.multiple_of(lo, 128)
-        delta_ref[:, pl.ds(lo, HALF_SLOTS)] = dall[pl.ds(lo, HALF_SLOTS), :].astype(F32).T[0:TALL].astype(BF16)
-
-    turn(mine_from)
+    for t in chains:
+        for k in range(3):
+            out_first[t][k].wait_recv()
+            rows = at_rows(dall, mine_from + lax.rem(first + 3 - k, 4) * FIRST_PART + t * CHAIN, CHAIN)
+            swaps.append(send(rows, rows, core_mate))
+            swaps[-1].start()
+
+    def turn(lo, size):
+        rows = dall[lo : lo + HALF_SLOTS, :].astype(F32).T[:, 0:size]
+        rtab[:, lo : lo + size] = rtab[:, lo : lo + size] + rows[0:W]
+        mean_ref[0:1, lo : lo + size] = rows[W : W + 1] + rows[W + 1 : W + 2]
+
+    halves = ((0, HALF_SLOTS), (HALF_SLOTS, RELS - HALF_SLOTS))
+    for c in range(2):
+        pl.when(core == c)(functools.partial(turn, *halves[c]))
     for copy in swaps:
         copy.wait_recv()
-    turn((1 - core) * HALF_SLOTS)
+    for c in range(2):
+        pl.when(core == c)(functools.partial(turn, *halves[1 - c]))
 
     for copy in [ask0, ask1, rows_out0, rows_out1] + combs + backs0 + backs0_y + backs1 + drel_sends:
         copy.wait_send()
     for group in shares0 + pass_on + shares1[0] + shares1[1]:
         for copy in group:
             copy.wait_send()
-    for copy in firsts + seconds + out_second + out_first + swaps:
-        copy.wait_send()
+    for group in firsts + seconds + out_second + out_first + [swaps]:
+        for copy in group:
+            copy.wait_send()
     for k in range(1, 8):
         pl.when(third(k)[0])(thirds[k - 1].wait_send)
 
@@ -467,52 +510,47 @@
 OWN_PIECES = ((0, 104), (104, 104), (208, 96), (304, 96))
 
 
-def finish(own, own_state, delta, rtab, rstate, ent_hbm, est_ref, rel_hbm, nstate, total, sem):
-    def pieces(source, target, first):
-        return [
-            pltpu.make_async_copy(source.at[pl.ds(lo, size), :], target.at[pl.ds(lo, size), :], sem.at[first + k])
-            for k, (lo, size) in enumerate(OWN_PIECES)
-        ]
-
-    stores, rel_stores = pieces(own, ent_hbm, 0), pieces(total, rel_hbm, 4)
+def finish(own, own_state, relations, mean, rstate, ent_hbm, est_ref, rel_hbm, nstate, sem):
+    stores = [
+        pltpu.make_async_copy(source.at[pl.ds(lo, size), :], target.at[pl.ds(lo, size), :], sem.at[first + k])
+        for source, target, first in ((own, ent_hbm, 0), (relations, rel_hbm, 4))
+        for k, (lo, size) in enumerate(OWN_PIECES)
+    ]
     for store in stores:
         store.start()
-    for k, (lo, size) in enumerate(OWN_PIECES):
-        at = slice(lo, lo + size)
-        total[at, :] = rtab[at, :] + delta[at, 0:RELS].astype(F32)
-        rel_stores[k].start()
     est_ref[...] = own_state[...]
-    tail = delta[W:TALL, :].astype(F32)
-    mean = tail[0:1, :] + tail[1:2, :]
-    nstate[...] = rstate[...] + mean.reshape(SLOTS)[:RELS]
-    for store in stores + rel_stores:
+    nstate[...] = rstate[...] + mean[0:1, :].reshape(SLOTS)[:RELS]
+    for store in stores:
         store.wait()
 
 
 def per_device(
     entity_table, entity_state, relation_table, relation_state, source_rows, target_rows, relation_ids, live_counts
 ):
-    vmem, smem = pl.BlockSpec(memory_space=pltpu.VMEM), pl.BlockSpec(memory_space=pltpu.SMEM)
+    vmem, ids = pl.BlockSpec(memory_space=pltpu.VMEM), pltpu.VMEM((2, 1, GROUP), I32)
     anywhere = pl.BlockSpec(memory_space=pl.ANY)
     contributions = pltpu.VMEM((W, 8 * GROUP), BF16)
     blocks = pltpu.VMEM((2, W, GROUP), BF16)
     block_f, state_row = pltpu.VMEM((W, GROUP), F32), pltpu.VMEM((8, GROUP), F32)
-    relations = relation_table.T
-    own, own_state, delta = pl.pallas_call(
+    own, own_state, new_relations, mean = pl.pallas_call(
         kernel,
         out_shape=(
             pltpu.VMEM((W, SHARE), F32),
             pltpu.VMEM((8, 128), F32),
-            pltpu.VMEM((TALL, SLOTS), BF16),
+            pltpu.VMEM((W, RELS), F32),
+            pltpu.VMEM((8, SLOTS), F32),
         ),
-        in_specs=[anywhere, anywhere, vmem, smem, vmem, vmem, vmem, smem],
-        out_specs=(vmem, vmem, vmem),
+        in_specs=[anywhere] * 8,
+        out_specs=(vmem, vmem, vmem, vmem),
         scratch_shapes=[
             pltpu.VMEM((W, ROWS), F32),
-            pltpu.VMEM((W, RELS), F32),
-            pltpu.VMEM((2 * W + 16, ROWS), BF16),
+            pltpu.VMEM((W + 16, ROWS), BF16),
             pltpu.VMEM((W, RELS), BF16),
             pltpu.VMEM((16, ROWS), F32),
+            pltpu.VMEM((ROWS // 128, 128), F32),
+            pltpu.SMEM((RELS,), F32),
+            ids, ids, ids,
+            pltpu.SMEM((2,), I32),
             pltpu.VMEM((8, GROUP), I32),
             pltpu.VMEM((2, 8, GROUP), I32),
             pltpu.VMEM((4, 8, GROUP), I32),
@@ -529,13 +567,13 @@
             pltpu.VMEM((3, FIRST_PART, WIDE), BF16),
             pltpu.VMEM((FIRST_PART, WIDE), F32),
             pltpu.VMEM((FIRST_PART, WIDE), BF16),
-            pltpu.VMEM((3, SECOND_PART, WIDE), BF16),
-            pltpu.VMEM((SECOND_PART, WIDE), F32),
-            pltpu.VMEM((SECOND_PART, WIDE), BF16),
+            pltpu.VMEM((3, CHAINS * THIRD_PART, WIDE), BF16),
+            pltpu.VMEM((CHAINS * THIRD_PART, WIDE), F32),
+            pltpu.VMEM((CHAINS * THIRD_PART, WIDE), BF16),
             pltpu.VMEM((7, THIRD_PART, WIDE), BF16),
             pltpu.VMEM((THIRD_PART, 128), F32),
             pltpu.VMEM((SLOTS, WIDE), BF16),
-            pltpu.SemaphoreType.DMA((7,)),
+            pltpu.SemaphoreType.DMA((11,)),
             pltpu.SemaphoreType.DMA((SEMS,)),
             pltpu.SemaphoreType.DMA((SEMS,)),
         ],
@@ -543,7 +581,7 @@
             collective_id=0, has_side_effects=True, vmem_limit_bytes=58 * 1024 * 1024
         ),
     )(
-        entity_table.T, relations, entity_state.reshape(ROWS // 128, 128), relation_state,
+        entity_table.T, relation_table.T, entity_state.reshape(ROWS // 128, 128), relation_state,
         source_rows, target_rows, relation_ids, live_counts.reshape(-1),
     )
     own, own_state, new_relations, new_state = pl.pallas_call(
@@ -557,11 +595,10 @@
         in_specs=[vmem, vmem, vmem, vmem, vmem],
         out_specs=(anywhere, vmem, anywhere, vmem),
         scratch_shapes=[
-            pltpu.VMEM((W, RELS), F32),
             pltpu.SemaphoreType.DMA((8,)),
         ],
         compiler_params=pltpu.CompilerParams(vmem_limit_bytes=12 * 1024 * 1024),
-    )(own, own_state, delta, relations, relation_state)
+    )(own, own_state, new_relations, mean, relation_state)
     return own.T, own_state.reshape(-1), new_relations.T, new_state
 
 

time: 89.7 us -> 83.7 us (0.933)
  Pallas kernels: 88.8 us -> 82.8 us
    pallas_call x1, Pallas kernels: 86.2 us -> 80.2 us  [per_device(): pl.pallas_call(kernel, out_shape=(pltpu.VMEM((W, SHARE), F32), pltpu.VMEM...]
where the time goes in v4:
time: 83.7 us; the launch traced here: 83.6 us
  Pallas kernels  82.8 us (99%)
    pallas_call x1, Pallas kernels, per_device(): pl.pallas_call(kernel, out_shape=(pltpu.VMEM((W, SHARE), F32), pltpu.VMEM...  80.2 us
    pallas_call x1, Pallas kernels, per_device(): pl.pallas_call(finish, out_shape=(jax.ShapeDtypeStruct((W, SHARE), F32),...  2.57 us

profile of v4, /device:TPU:1, one launch (start us, length us, event | category | flops | bytes accessed | tf_op | source)
XLA Modules:
  0.0 83.6 jit_solution(3092503344106788602)
XLA Ops:
  0.6 0.0 copy-start
  0.6 80.2 %shard_map.111 = (f32[400,1024]{1,0:T(8,128)S(1)}, f32[8,128]{1,0:T(8,128)S(1)}, f32[400,1300]{1,0:T(8,128)S(1)}, f32[8,1536]{1,0:T(8,128)S(1)}) custom-call(f32[400,4096]{1,0:T(8,128)} %bitcast.7, f32[400,1300]{1,0:T(8,128)} %bitcast.8, f32[32,128]{1,0:T(8,128)} %bitcast.9, f32[1300]{0:T(1024)} %rstate.1, s32[2,1,256]{2,1,0:T(1,128)} %src_hbm.1, ...), custom_call_target="tpu_custom_call" | custom-call | tf_op jit(solution)/shard_map/pallas_call | solution.py:535
  80.9 0.0 copy-done
  80.9 2.6 %shard_map.112 = (f32[400,1024]{1,0:T(8,128)}, f32[8,128]{1,0:T(8,128)}, f32[400,1300]{1,0:T(8,128)}, f32[1300]{0:T(1024)}) custom-call(f32[400,1024]{1,0:T(8,128)S(1)} %get-tuple-element.12.own, f32[8,128]{1,0:T(8,128)S(1)} %get-tuple-element.13.own_state, f32[400,1300]{1,0:T(8,128)S(1)} %get-tuple-element.14.relations, ...), custom_call_target="tpu_custom_call" | custom-call | tf_op jit(solution)/shard_map/pallas_call | solution.py:587
Async XLA Ops:
  0.6 80.2 %copy-start = (f32[1300]{0:T(1024)S(1)}, f32[1300]{0:T(1024)}, u32[]{:S(2)}) copy-start(f32[1300]{0:T(1024)} %rstate.1) | copy-start | bytes 15604

commit v5 on v4

--- a/solution.py
+++ b/solution.py
@@ -372,10 +372,7 @@
     start(firsts[1] + firsts[2])
 
     back[1] = mat(queries_b, coeffs.astype(BF16)).astype(BF16)
-    start(backs1)
     c1[:, mine_at(0)] = conj_product(d_queries, rel1[...]).astype(BF16)
-    for group in shares1[0]:
-        start(group[:2])
 
     seconds = [
         [
@@ -397,6 +394,9 @@
         qsum[at, :] = total
         qsend[at, :] = total.astype(BF16)
         start(seconds[t])
+    start(backs1)
+    for group in shares1[0]:
+        start(group[:2])
 
     thirds = [
         send(at_rows(rsend, third(k)[1] * THIRD_PART, THIRD_PART), zin.at[k - 1], z_peers[k - 1])
@@ -412,12 +412,6 @@
         rsend[at, :] = total.astype(BF16)
         for k in range(1, 8):
             pl.when(holds(k, t))(thirds[k - 1].start)
-
-    for k in range(len(PIECES)):
-        backs1[k].wait_recv()
-        start(shares1[1][k][:2])
-        shares1[0][k][1].wait_recv()
-        shares1[0][k][2].start()
 
     third_rows = at_rows(dall, third_row, THIRD_PART)
     out_z = [send(third_rows, third_rows, device) for device in z_peers]
@@ -436,21 +430,17 @@
         third_rows[...] = delta.astype(BF16)
         start(out_z)
 
-    for group in shares1[1]:
-        group[1].wait_recv()
-        group[2].start()
-    for kind in range(2):
-        for group in shares1[kind]:
-            group[0].wait_recv()
-            group[2].wait_recv()
-
+    for k in range(len(PIECES)):
+        backs1[k].wait_recv()
+        start(shares1[1][k][:2])
+        shares1[0][k][1].wait_recv()
+        shares1[0][k][2].start()
     def own_tiles(tiles):
         for tile in tiles:
             at = slice(tile * GROUP, (tile + 1) * GROUP)
             grads = summed(c1, 0, 1, tile_ids(tile)) + summed(c1, 1, 3, tile_ids(tile))
             own[:, at], own_st[0:1, at] = adagrad(own[:, at], own_st[0:1, at], grads)
 
-    own_tiles((0,))
     out_second, out_first, swaps = [], [], []
     for t in chains:
         for k in range(1, 8):
@@ -458,7 +448,9 @@
         rows = at_rows(dall, first_row + t * CHAIN + second * THIRD_PART, THIRD_PART)
         out_second.append([send(rows, rows, device) for device in second_peers])
         start(out_second[t])
-    own_tiles((1,))
+    for group in shares1[1]:
+        group[1].wait_recv()
+        group[2].start()
     for t in chains:
         for copy in out_second[t]:
             copy.wait_recv()
@@ -467,7 +459,11 @@
         start(out_first[t])
         swaps.append(send(rows, rows, core_mate))
         swaps[t].start()
-    own_tiles((2, 3))
+    for kind in range(2):
+        for group in shares1[kind]:
+            group[0].wait_recv()
+            group[2].wait_recv()
+    own_tiles((0, 1, 2, 3))
     for k in range(8):
         est_ref[k : k + 1, :] = own_st[0:1, k * 128 : (k + 1) * 128]
     for t in chains:

time: 83.7 us -> 81.6 us (0.975)
  Pallas kernels: 82.8 us -> 80.7 us
    pallas_call x1, Pallas kernels: 80.2 us -> 78.2 us  [per_device(): pl.pallas_call(kernel, out_shape=(pltpu.VMEM((W, SHARE), F32), pltpu.VMEM...]
where the time goes in v5:
time: 81.6 us
  Pallas kernels  80.7 us (99%)
  between operations  0.82 us (1%)
    pallas_call x1, Pallas kernels, per_device(): pl.pallas_call(kernel, out_shape=(pltpu.VMEM((W, SHARE), F32), pltpu.VMEM...  78.2 us
    pallas_call x1, Pallas kernels, per_device(): pl.pallas_call(finish, out_shape=(jax.ShapeDtypeStruct((W, SHARE), F32),...  2.57 us

profile of v5, /device:TPU:1, one launch (start us, length us, event | category | flops | bytes accessed | tf_op | source)
XLA Modules:
  0.0 81.6 jit_solution(5447305354305421716)
XLA Ops:
  0.6 0.0 copy-start
  0.6 78.2 %shard_map.111 = (f32[400,1024]{1,0:T(8,128)S(1)}, f32[8,128]{1,0:T(8,128)S(1)}, f32[400,1300]{1,0:T(8,128)S(1)}, f32[8,1536]{1,0:T(8,128)S(1)}) custom-call(f32[400,4096]{1,0:T(8,128)} %bitcast.7, f32[400,1300]{1,0:T(8,128)} %bitcast.8, f32[32,128]{1,0:T(8,128)} %bitcast.9, f32[1300]{0:T(1024)} %rstate.1, s32[2,1,256]{2,1,0:T(1,128)} %src_hbm.1, ...), custom_call_target="tpu_custom_call" | custom-call | tf_op jit(solution)/shard_map/pallas_call | solution.py:531
  78.8 0.0 copy-done
  78.8 2.6 %shard_map.112 = (f32[400,1024]{1,0:T(8,128)}, f32[8,128]{1,0:T(8,128)}, f32[400,1300]{1,0:T(8,128)}, f32[1300]{0:T(1024)}) custom-call(f32[400,1024]{1,0:T(8,128)S(1)} %get-tuple-element.12.own, f32[8,128]{1,0:T(8,128)S(1)} %get-tuple-element.13.own_state, f32[400,1300]{1,0:T(8,128)S(1)} %get-tuple-element.14.relations, ...), custom_call_target="tpu_custom_call" | custom-call | tf_op jit(solution)/shard_map/pallas_call | solution.py:583
Async XLA Ops:
  0.6 78.2 %copy-start = (f32[1300]{0:T(1024)S(1)}, f32[1300]{0:T(1024)}, u32[]{:S(2)}) copy-start(f32[1300]{0:T(1024)} %rstate.1) | copy-start | bytes 15604

commit v6 on v5

--- a/solution.py
+++ b/solution.py
@@ -282,25 +282,6 @@
         turned = columns(comb[b])
         for q in range(4):
             cid[q, b * GROUP : (b + 1) * GROUP, :] = turned[:, q : q + 1]
-    for k in range(len(PIECES)):
-        shares0[k][1].wait_recv()
-        shares0[k][2].start()
-
-    for group in shares0:
-        group[0].wait_recv()
-        group[2].wait_recv()
-
-    def summed(ref, kind, q, ids):
-        return mat(ref[:, kind * 1024 : (kind + 1) * 1024], indicator(cid[q] == ids.astype(F32)))
-
-    own_first = rep * SHARE
-
-    def tile_ids(tile):
-        return iota((1, GROUP), 1) + (own_first + tile * GROUP)
-
-    gsum[:, 0:256] = summed(c0, 1, 2, req1_ids)
-    gsum[:, 256:512] = summed(c0, 1, 2, src1_ids)
-
     def relation_part(t, rows, rid, lo):
         ids = iota((FIRST_PART, 1), 0) + (mine_from + lo)
         return mat(indicator(ids == rid), rows[t])
@@ -311,12 +292,28 @@
             0, dmate, comb[core_rep, 4:5, :], lo
         )
     rel1[...] = lookup(rtab_b[...], msg[5:6, :])
+
     for k in range(len(PIECES)):
+        shares0[k][1].wait_recv()
+        shares0[k][2].start()
         backs0[k].wait_recv()
         pass_on[k][0].start()
         backs0_y[k].wait_recv()
         pass_on[k][1].start()
-
+    for group in shares0:
+        group[0].wait_recv()
+        group[2].wait_recv()
+
+    def summed(ref, kind, q, ids):
+        return mat(ref[:, kind * 1024 : (kind + 1) * 1024], indicator(cid[q] == ids.astype(F32)))
+
+    own_first = rep * SHARE
+
+    def tile_ids(tile):
+        return iota((1, GROUP), 1) + (own_first + tile * GROUP)
+
+    gsum[:, 0:256] = summed(c0, 1, 2, req1_ids)
+    gsum[:, 256:512] = summed(c0, 1, 2, src1_ids)
     for group in pass_on:
         for copy in group:
             copy.wait_recv()
@@ -333,11 +330,14 @@
     queries = product(src1[...], rel1[...])
     queries_row, queries_b = queries.T.astype(BF16), queries.astype(BF16)
 
-    for tile in range(SHARE // GROUP):
+    def first_update(tile):
         at = slice(tile * GROUP, (tile + 1) * GROUP)
         grads = summed(c0, 0, 0, tile_ids(tile)) + summed(c0, 1, 2, tile_ids(tile))
         rows = tab[:, pl.ds(pl.multiple_of(own_first + tile * GROUP, GROUP), GROUP)]
         own[:, at], own_st[0:1, at] = adagrad(rows, own_st[0:1, at], grads)
+
+    for tile in (0, 1):
+        first_update(tile)
 
     rows_out1.wait_recv()
     backs1, shares1 = back_copies(1, c1, other, 1), share_copies(c1)
@@ -373,6 +373,9 @@
 
     back[1] = mat(queries_b, coeffs.astype(BF16)).astype(BF16)
     c1[:, mine_at(0)] = conj_product(d_queries, rel1[...]).astype(BF16)
+
+    for tile in (2, 3):
+        first_update(tile)
 
     seconds = [
         [

time: 81.6 us -> 82.6 us (1.012)
  Pallas kernels: 80.7 us -> 81.7 us
    pallas_call x1, Pallas kernels: 78.2 us -> 79.1 us  [per_device(): pl.pallas_call(kernel, out_shape=(pltpu.VMEM((W, SHARE), F32), pltpu.VMEM...]
where the time goes in v6:
time: 82.6 us; the launch traced here: 82.5 us
  Pallas kernels  81.7 us (99%)
    pallas_call x1, Pallas kernels, per_device(): pl.pallas_call(kernel, out_shape=(pltpu.VMEM((W, SHARE), F32), pltpu.VMEM...  79.1 us
    pallas_call x1, Pallas kernels, per_device(): pl.pallas_call(finish, out_shape=(jax.ShapeDtypeStruct((W, SHARE), F32),...  2.57 us

profile of v6, /device:TPU:1, one launch (start us, length us, event | category | flops | bytes accessed | tf_op | source)
XLA Modules:
  0.0 82.5 jit_solution(10362384410905307851)
XLA Ops:
  0.6 0.0 copy-start
  0.6 79.1 %shard_map.111 = (f32[400,1024]{1,0:T(8,128)S(1)}, f32[8,128]{1,0:T(8,128)S(1)}, f32[400,1300]{1,0:T(8,128)S(1)}, f32[8,1536]{1,0:T(8,128)S(1)}) custom-call(f32[400,4096]{1,0:T(8,128)} %bitcast.7, f32[400,1300]{1,0:T(8,128)} %bitcast.8, f32[32,128]{1,0:T(8,128)} %bitcast.9, f32[1300]{0:T(1024)} %rstate.1, s32[2,1,256]{2,1,0:T(1,128)} %src_hbm.1, ...), custom_call_target="tpu_custom_call" | custom-call | tf_op jit(solution)/shard_map/pallas_call | solution.py:534
  79.8 0.0 copy-done
  79.8 2.6 %shard_map.112 = (f32[400,1024]{1,0:T(8,128)}, f32[8,128]{1,0:T(8,128)}, f32[400,1300]{1,0:T(8,128)}, f32[1300]{0:T(1024)}) custom-call(f32[400,1024]{1,0:T(8,128)S(1)} %get-tuple-element.12.own, f32[8,128]{1,0:T(8,128)S(1)} %get-tuple-element.13.own_state, f32[400,1300]{1,0:T(8,128)S(1)} %get-tuple-element.14.relations, ...), custom_call_target="tpu_custom_call" | custom-call | tf_op jit(solution)/shard_map/pallas_call | solution.py:586
Async XLA Ops:
  0.6 79.2 %copy-start = (f32[1300]{0:T(1024)S(1)}, f32[1300]{0:T(1024)}, u32[]{:S(2)}) copy-start(f32[1300]{0:T(1024)} %rstate.1) | copy-start | bytes 15604
